TPU v7x, 512 devices: a whole 4x4x16 slice. The times are simulated.
512 devices in a mesh: dp: 32 (over z, core), proto: 16 (over x, y).
Axes of the slice: x: 4, y: 4, z: 16, core: 2. Of those that a mesh axis runs over, the one named last changes fastest.
Arguments:
- embeddings: bfloat16 [49152, 1536], P('dp'), may hold values from -13 to 13
- centroids: bfloat16 [8192, 1536], P('proto', 'dp'), may hold values from -6 to 6
Outputs:
- new_centroids: float32 [1536, 8192], P('dp', 'proto')
- cluster_mass: float32 [8192], P('proto')
All inputs are finite; a program needn't handle non-finite values.
Results may differ from a plain program's by a relative error of at most 0.00031.
Values may be sent and summed in bfloat16 or wider, within the bound.
A program may use at most 64 MiB of HBM per device.

v0:
```python
import jax
import jax.numpy as jnp
from jax import lax
from jax.sharding import PartitionSpec as P

SWEEPS = 3


logit_scale = 40.0


def per_device(embeddings, centroids):
    values = embeddings.astype(jnp.float32)
    unit_rows = (values / jnp.sqrt(jnp.sum(values * values, axis=1, keepdims=True) + 1e-06)).astype(
        jnp.bfloat16
    )
    local_rows = unit_rows.shape[0]
    local_cent = centroids.shape[0]
    total_rows = local_rows * lax.axis_size("dp")
    total_cent = local_cent * lax.axis_size("proto")
    block_piece = lax.all_gather(centroids, "dp", axis=1, tiled=True)
    scored = lax.dot_general(
        unit_rows, block_piece, (((1,), (1,)), ((), ())), preferred_element_type=jnp.float32
    )
    squares = jnp.sum(jnp.square(block_piece.astype(jnp.float32)), axis=1)
    inv_norm = 1.0 / jnp.sqrt(squares + 1e-06)
    exp_scores = jnp.exp(logit_scale * scored * inv_norm[None, :])
    row_scale = jnp.ones((local_rows,), jnp.float32)
    col_scale = jnp.ones((local_cent,), jnp.float32)
    for sweep_index in range(SWEEPS):
        col_total = lax.psum(jnp.sum(exp_scores * row_scale[:, None], axis=0), "dp")
        col_scale = 1.0 / (total_cent * col_total)
        row_total = lax.psum(jnp.sum(exp_scores * col_scale[None, :], axis=1), "proto")
        row_scale = 1.0 / (total_rows * row_total)
    assign = total_rows * exp_scores * row_scale[:, None] * col_scale[None, :]
    cluster_mass = lax.psum(jnp.sum(assign, axis=0), "dp") * (total_cent / total_rows)
    weights = assign.astype(jnp.bfloat16)
    feat_rows = unit_rows.shape[1] // lax.axis_size("dp")
    local_sums = lax.dot_general(
        unit_rows, weights, (((0,), (0,)), ((), ())), preferred_element_type=jnp.float32
    )
    whole_sums = lax.psum(local_sums, "dp")
    lengths = jnp.sum(whole_sums * whole_sums, axis=0, keepdims=True)
    own_block = lax.dynamic_slice_in_dim(whole_sums, lax.axis_index("dp") * feat_rows, feat_rows, 0)
    new_centroids = own_block / jnp.sqrt(lengths + 1e-06)
    return (new_centroids, cluster_mass)


def solution(mesh):
    return jax.shard_map(
        per_device,
        mesh=mesh,
        in_specs=(P("dp", None), P("proto", "dp")),
        out_specs=(P("dp", "proto"), P("proto")),
        check_vma=False,
    )
```

profile of v0, /device:TPU:1, one launch (start us, length us, event | category | flops | bytes accessed | tf_op | source)
XLA Modules:
  0.0 575.9 jit_solution(4089868178512826132)
XLA Ops:
  7.2 0.0 all-gather.2.cloned.1.call-start
  7.2 0.7 all-gather.2.cloned.1.call-update
  7.9 0.0 all-reduce.2.cloned.1.call-start
  7.9 0.0 copy-start
  8.0 3.5 fusion
  11.4 0.3 copy-done
  11.7 4.0 fusion.1
  15.7 71.5 %all-gather.2.cloned.1.call-done = bf16[512,1536]{0,1:T(8,128)(2,1)} async-done(((bf16[512,48]{0,1:T(8,128)(2,1)}), bf16[512,1536]{0,1:T(8,128)(2,1)}) %all-gather.2.cloned.1.call-update) | async-done | bytes 1572880 | tf_op jit(solution)/shard_map/all_gather | solution.py:21
  87.2 1.8 multiply_reduce_fusion.6
  89.0 4.9 fusion.9
  94.0 45.4 %psum.56 = f32[512]{0:T(512)S(1)} all-reduce(f32[512]{0:T(512)S(1)} %get-tuple-element.2), channel_id=1, replica_groups=mesh['dp'=32,'proto'=16] {'dp'}, use_global_device_ids=true, to_apply=%region_3.0 | all-reduce | flops 512 | bytes 4096 | tf_op jit(solution)/shard_map/psum | solution.py:31
  139.4 0.3 multiply_reduce_fusion.5
  139.7 34.0 %psum.57 = f32[1536]{0:T(1024)S(1)} all-reduce(f32[1536]{0:T(1024)S(1)} %multiply_reduce_fusion.5), channel_id=1, replica_groups=mesh['dp'=32,'proto'=16] {'proto'}, use_global_device_ids=true, to_apply=%region_5.0 | all-reduce | flops 1536 | bytes 12288 | tf_op jit(solution)/shard_map/psum | solution.py:33
  173.7 0.3 multiply_reduce_fusion.4
  174.0 55.0 %psum.58 = f32[512]{0:T(512)S(1)} all-reduce(f32[512]{0:T(512)S(1)} %multiply_reduce_fusion.4), channel_id=1, replica_groups=mesh['dp'=32,'proto'=16] {'dp'}, use_global_device_ids=true, to_apply=%region_7.0 | all-reduce | flops 512 | bytes 4096 | tf_op jit(solution)/shard_map/psum | solution.py:31
  229.1 0.3 multiply_reduce_fusion.3
  229.3 29.3 %psum.59 = f32[1536]{0:T(1024)S(1)} all-reduce(f32[1536]{0:T(1024)S(1)} %multiply_reduce_fusion.3), channel_id=1, replica_groups=mesh['dp'=32,'proto'=16] {'proto'}, use_global_device_ids=true, to_apply=%region_9.0 | all-reduce | flops 1536 | bytes 12288 | tf_op jit(solution)/shard_map/psum | solution.py:33
  258.7 0.3 multiply_reduce_fusion.2
  259.0 52.4 %psum.60 = f32[512]{0:T(512)S(1)} all-reduce(f32[512]{0:T(512)S(1)} %multiply_reduce_fusion.2), channel_id=1, replica_groups=mesh['dp'=32,'proto'=16] {'dp'}, use_global_device_ids=true, to_apply=%region_11.0 | all-reduce | flops 512 | bytes 4096 | tf_op jit(solution)/shard_map/psum | solution.py:31
  311.4 0.3 multiply_reduce_fusion.1
  311.7 31.1 %psum.61 = f32[1536]{0:T(1024)S(1)} all-reduce(f32[1536]{0:T(1024)S(1)} %multiply_reduce_fusion.1), channel_id=1, replica_groups=mesh['dp'=32,'proto'=16] {'proto'}, use_global_device_ids=true, to_apply=%region_13.0 | all-reduce | flops 1536 | bytes 12288 | tf_op jit(solution)/shard_map/psum | solution.py:33
  342.9 6.7 %fusion.5 = f32[1536,512]{1,0:T(8,128)} fusion(bf16[1536,1536]{1,0:T(8,128)(2,1)} %fusion.1, f32[1536,512]{1,0:T(8,128)S(1)} %get-tuple-element.3, f32[1536]{0:T(1024)S(1)} %divide_multiply_fusion, f32[512]{0:T(512)S(1)} %multiply_divide_fusion.2), kind=kOutput, calls=%fused_computation.16 | convolution fusion | flops 2418278400 | bytes 11018240 | tf_op jit(solution)/shard_map/dot_general | solution.py:39
  349.6 0.0 all-reduce.2.cloned.1.call-update
  349.6 0.4 fusion.3
  350.0 52.7 %psum.63 = f32[512]{0:T(512)S(1)} all-reduce(f32[512]{0:T(512)S(1)} %fusion.3), channel_id=1, replica_groups=mesh['dp'=32,'proto'=16] {'dp'}, use_global_device_ids=true, to_apply=%region_17.0 | all-reduce | flops 512 | bytes 4096 | tf_op jit(solution)/shard_map/psum | solution.py:36
  402.7 0.6 broadcast_multiply_fusion
  403.3 162.0 %all-reduce.2.cloned.1.call-done = f32[1536,512]{1,0:T(8,128)} async-done(((f32[1536,512]{1,0:T(8,128)}), f32[1536,512]{1,0:T(8,128)}) %all-reduce.2.cloned.1.call-update) | async-done | bytes 3145744 | tf_op jit(solution)/shard_map/psum | solution.py:42
  565.3 2.2 multiply_reduce_fusion
  567.5 1.6 dynamic-slice_divide_fusion
  (9 shorter events, 0.1 us)
Async XLA Ops:
  7.2 80.0 %all-gather.2.cloned.1.call-start = ((), (), s32[]{:S(2)}) async-start(), calls=%async_computation | async-start | bytes 1622016 | tf_op jit(solution)/shard_map/all_gather | solution.py:21
  7.9 557.4 %all-reduce.2.cloned.1.call-start = ((), (), s32[]{:S(2)}) async-start(), calls=%async_computation.1 | async-start | bytes 6291456 | tf_op jit(solution)/shard_map/psum | solution.py:42
  7.9 3.8 copy-start
Sparse Core Ops, SparseCore 0:
  10.1 77.0 all-gather.1
  349.7 215.5 all-reduce.1
where the time goes:
time: 576 us
  blocking collectives  300 us (52%)
  waiting for transfers between devices  234 us (41%)
  other arithmetic  15.5 us (3%)
  between operations  14.1 us (2%)
  matrix products  11.7 us (2%)
    psum x1, waiting for transfers between devices, per_device(): whole_sums = lax.psum(local_sums, 'dp')  162 us
    psum x3, blocking collectives, per_device(): col_total = lax.psum(jnp.sum(exp_scores * row_scale[:, None], axis=0), 'dp')  153 us
    psum x3, blocking collectives, per_device(): lax.psum(jnp.sum(exp_scores * col_scale[None, :], axis=1), 'proto')  94.5 us
    all_gather x1, waiting for transfers between devices, per_device(): block_piece = lax.all_gather(centroids, 'dp', axis=1, tiled=True)  71.5 us
    psum x1, blocking collectives, per_device(): lax.psum(jnp.sum(assign, axis=0), 'dp') * (total_cent / total_rows)  52.7 us
  transfers between devices with their start and end apart: 2, of which 2 were waited for; matrix products, arithmetic and copies ran while one was open for 1% of the time, Pallas kernels for 0%

commit v1 on v0

v1 whole, which is shorter than its diff:
```python
import functools

import jax
import jax.numpy as jnp
from jax import lax
from jax.experimental import pallas as pl
from jax.experimental.pallas import tpu as pltpu
from jax.sharding import PartitionSpec as P

SWEEPS = 3
LOGIT_SCALE = 40.0
F32, BF16 = jnp.float32, jnp.bfloat16
MESH = pl.DeviceIdType.MESH
GROUP = 8


def dot(a, b, dims):
    return lax.dot_general(a, b, (dims, ((), ())), preferred_element_type=F32)


def kernel(sizes, emb, cen, out, mass_out, x, ut, ct, e, w, s, cvec, rvec, cpart, col_a, col_b, row_x,
           fin_a, fin_b, sib, ring, sem_in, sib_sem, g_send, g_recv, gs_send, gs_recv, ca_sem, cb_sem, rx_sem,
           fa_sem, fb_sem, sx_send, sx_recv, r_send, r_recv):
    n_dp, n_proto, rows, feat, cent = sizes
    nz = n_dp // 2
    half = nz // 2
    own = feat // n_dp
    n_rows = rows * n_dp
    n_cent = cent * n_proto
    levels = n_dp // GROUP
    lanes = 128

    d = lax.axis_index("dp")
    p = lax.axis_index("proto")
    z, c = d // 2, d % 2
    other = d + 1 - 2 * c
    right = ((z + 1) % nz) * 2 + c
    left = ((z + nz - 1) % nz) * 2 + c
    base = (d // GROUP) * GROUP

    def in_group(j):
        return base + (d - base + j) % GROUP

    def in_level(j):
        return (d + GROUP * j) % n_dp

    barrier = pltpu.get_barrier_semaphore()
    for j in range(1, GROUP):
        pl.semaphore_signal(barrier, inc=1, device_id={"dp": in_group(j)}, device_id_type=MESH)
    for j in range(1, levels):
        pl.semaphore_signal(barrier, inc=1, device_id={"dp": in_level(j)}, device_id_type=MESH)
    for t in (left, right):
        pl.semaphore_signal(barrier, inc=1, device_id={"dp": t}, device_id_type=MESH)

    def greet(j, carry):
        pl.semaphore_signal(barrier, inc=1, device_id={"proto": (p + j) % n_proto}, device_id_type=MESH)
        return carry

    lax.fori_loop(1, n_proto, greet, 0)

    load = pltpu.make_async_copy(emb, x, sem_in)
    load.start()

    def eye(n):
        return (
            lax.broadcasted_iota(jnp.int32, (n, n), 0) == lax.broadcasted_iota(jnp.int32, (n, n), 1)
        ).astype(BF16)

    def block_rows(o, core):
        return pl.ds(pl.multiple_of((o * 2 + core) * own, own), own)

    ct[block_rows(z, c), :] = dot(eye(own), cen[...], ((1,), (1,))).astype(BF16)
    pl.semaphore_wait(barrier, (GROUP - 1) + (levels - 1) + 2 + (n_proto - 1))

    def hop(o, way, step):
        return pltpu.make_async_remote_copy(
            src_ref=ct.at[block_rows(o, c)], dst_ref=ct.at[block_rows(o, c)],
            send_sem=g_send.at[way, step], recv_sem=g_recv.at[way, step],
            device_id={"dp": right if way == 0 else left}, device_id_type=MESH)

    def across(o, slot):
        return pltpu.make_async_remote_copy(
            src_ref=ct.at[block_rows(o, c)], dst_ref=ct.at[block_rows(o, c)],
            send_sem=gs_send.at[slot], recv_sem=gs_recv.at[slot],
            device_id={"dp": other}, device_id_type=MESH)

    sent = []
    for desc in (hop(z, 0, 0), hop(z, 1, 0), across(z, 0)):
        desc.start()
        sent.append(desc)

    load.wait()
    tile = 256
    eye_t = eye(tile)

    def prepare(b):
        at = pl.ds(b * tile, tile)
        v = x[at, :].astype(F32)
        u = (v / jnp.sqrt(jnp.sum(v * v, axis=1, keepdims=True) + 1e-06)).astype(BF16)
        x[at, :] = u
        for f in range(feat // tile):
            ut[pl.ds(f * tile, tile), at] = dot(
                eye_t, u[:, f * tile:(f + 1) * tile], ((1,), (1,))).astype(BF16)

    for step in range(half):
        if step < rows // tile:
            prepare(step)
        for way in (0, 1):
            last = half - 1 if way == 0 else half - 2
            if step > last:
                continue
            o = (z - 1 - step + nz) % nz if way == 0 else (z + 1 + step) % nz
            hop(o, way, step).wait_recv()
            if step < last:
                desc = hop(o, way, step + 1)
                desc.start()
                sent.append(desc)
            desc = across(o, 1 + 2 * step + way)
            desc.start()
            sent.append(desc)
    for slot in range(nz):
        across(z, slot).wait_recv()
    for desc in sent:
        desc.wait_send()

    def square(b, acc):
        v = ct[pl.ds(pl.multiple_of(b * own, own), own), :].astype(F32)
        return acc + jnp.sum((v * v).reshape(own // 8, 8, cent), axis=0)

    squares = jnp.sum(lax.fori_loop(0, n_dp, square, jnp.zeros((8, cent), F32)), axis=0, keepdims=True)
    scale = LOGIT_SCALE * (1.0 / jnp.sqrt(squares + 1e-06))

    m_tile = rows // 4

    def score(b, acc):
        at = pl.ds(pl.multiple_of(b * m_tile, m_tile), m_tile)
        v = jnp.exp(dot(x[at, :], ct[...], ((1,), (0,))) * scale)
        e[at, :] = v
        return acc + jnp.sum(v.reshape(m_tile // 8, 8, cent), axis=0)

    cpart[...] = jnp.sum(lax.fori_loop(0, 4, score, jnp.zeros((8, cent), F32)), axis=0, keepdims=True)

    def exchange(buf, sem, n, target):
        def copy(j):
            return pltpu.make_async_remote_copy(
                src_ref=buf.at[0], dst_ref=buf.at[j], send_sem=sem.at[0], recv_sem=sem.at[1],
                device_id=target(j), device_id_type=MESH)

        def go(j, carry):
            copy(j).start()
            return carry

        lax.fori_loop(1, n, go, 0)
        whole = buf.at[pl.ds(1, n - 1)]
        done = pltpu.make_async_remote_copy(
            src_ref=whole, dst_ref=whole, send_sem=sem.at[0], recv_sem=sem.at[1],
            device_id=target(1), device_id_type=MESH)
        done.wait_recv()
        done.wait_send()

    def total(buf, n, me):
        acc = buf[(me + n) % n]
        for src in range(1, n):
            acc = acc + buf[(me - src + n) % n]
        return acc

    def sum_dp(first, second, first_sem, second_sem):
        exchange(first, first_sem, GROUP, lambda j: {"dp": in_group(j)})
        second[0] = total(first, GROUP, d % GROUP)
        exchange(second, second_sem, levels, lambda j: {"dp": in_level(j)})
        return total(second, levels, d // GROUP)

    lane = lax.broadcasted_iota(jnp.int32, (8, lanes), 1)
    unit = 16

    def sweep(i, carry):
        col_a[i, 0] = cpart[...]
        col_total = sum_dp(col_a.at[i], col_b.at[i], ca_sem.at[i], cb_sem.at[i])
        cv = 1.0 / (n_cent * col_total)
        cvec[...] = cv
        cb = jnp.broadcast_to(cv, (8, cent))
        for h in range(2):
            def row_step(g, acc):
                for k in range(unit):
                    at = pl.multiple_of((h * (rows // 2)) + g * (unit * 8) + k * 8, 8)
                    q = e[pl.ds(at, 8), :] * cb
                    q = functools.reduce(lambda a, b: a + b,
                                         [q[:, t * lanes:(t + 1) * lanes] for t in range(cent // lanes)])
                    acc = jnp.where(lane == g * unit + k, jnp.sum(q, axis=1, keepdims=True), acc)
                return acc

            row_x[i, 0, h] = lax.fori_loop(0, rows // 16 // unit, row_step, jnp.zeros((8, lanes), F32))
        exchange(row_x.at[i], rx_sem.at[i], n_proto, lambda j: {"proto": (p + j) % n_proto})
        rv = 1.0 / (n_rows * total(row_x.at[i], n_proto, p))
        rvec[...] = rv

        acc = jnp.zeros((8, cent), F32)
        for h in range(2):
            def col_step(g, st):
                acc, r = st
                for k in range(unit):
                    at = pl.multiple_of((h * (rows // 2)) + g * (unit * 8) + k * 8, 8)
                    acc = acc + e[pl.ds(at, 8), :] * jnp.broadcast_to(r[:, k:k + 1], (8, cent))
                return acc, pltpu.roll(r, lanes - unit, 1)

            acc, _ = lax.fori_loop(0, rows // 16 // unit, col_step, (acc, rv[h]))
        cpart[...] = jnp.sum(acc, axis=0, keepdims=True)
        return carry

    lax.fori_loop(0, SWEEPS, sweep, 0)

    nc = jnp.broadcast_to(n_rows * cvec[...], (8, cent))
    for h in range(2):
        def weigh(g, r):
            for k in range(0, unit, 2):
                at = pl.multiple_of((h * (rows // 2)) + g * (unit * 8) + k * 8, 16)
                pair = [
                    e[pl.ds(at + 8 * m, 8), :] * jnp.broadcast_to(r[:, k + m:k + m + 1], (8, cent)) * nc
                    for m in range(2)
                ]
                w[pl.ds(at, 16), :] = jnp.concatenate(pair, axis=0).astype(BF16)
            return pltpu.roll(r, lanes - unit, 1)

        lax.fori_loop(0, rows // 16 // unit, weigh, rvec[h])

    def gather_sums(b, carry):
        at = pl.ds(pl.multiple_of(b * m_tile, m_tile), m_tile)
        s[at, :] = dot(ut[at, :], w[...], ((1,), (0,)))
        return carry

    lax.fori_loop(0, 4, gather_sums, 0)

    order = [half]
    for q in range(1, half):
        order += [half - q, half + q]
    order += [0]

    def swap(rel):
        return pltpu.make_async_remote_copy(
            src_ref=s.at[block_rows((z + rel) % nz, 1 - c)], dst_ref=sib.at[rel],
            send_sem=sx_send.at[rel], recv_sem=sx_recv.at[rel],
            device_id={"dp": other}, device_id_type=MESH)

    for rel in order:
        swap(rel).start()

    wide = cent // 2
    flows = [(0, 0, half), (1, 1, half), (0, 1, half - 1), (1, 0, half - 1)]

    def link(way, part, t):
        return pltpu.make_async_remote_copy(
            src_ref=ring.at[way, part, t], dst_ref=ring.at[way, part, t + 1],
            send_sem=r_send.at[way, part, t], recv_sem=r_recv.at[way, part, t],
            device_id={"dp": right if way == 0 else left}, device_id_type=MESH)

    ready = set()
    moves = []
    for t in range(half):
        for way, part, hops in flows:
            if t >= hops:
                continue
            rel = hops - t if way == 0 else nz - (hops - t)
            if rel not in ready:
                swap(rel).wait_recv()
                ready.add(rel)
            cols = pl.ds(part * wide, wide)
            v = s[block_rows((z + rel) % nz, c), cols] + sib[rel, :, cols]
            if t > 0:
                link(way, part, t - 1).wait_recv()
                v = v + ring[way, part, t]
            ring[way, part, t] = v
            desc = link(way, part, t)
            desc.start()
            moves.append(desc)
    swap(0).wait_recv()
    for way, part, hops in flows:
        link(way, part, hops - 1).wait_recv()
    parts = []
    for part in range(2):
        cols = pl.ds(part * wide, wide)
        v = s[block_rows(z, c), cols] + sib[0, :, cols]
        for way, q, hops in flows:
            if q == part:
                v = v + ring[way, q, hops]
        parts.append(v)
    sums = jnp.concatenate(parts, axis=1)

    fin_a[0, :, 0:cent] = cpart[...]
    fin_a[0, :, cent:2 * cent] = jnp.sum(sums * sums, axis=0, keepdims=True)
    tot = sum_dp(fin_a, fin_b, fa_sem, fb_sem)
    mass_out[...] = n_cent * cvec[...] * tot[:, 0:cent]
    out[...] = sums / jnp.sqrt(tot[:, cent:2 * cent] + 1e-06)

    for rel in order:
        swap(rel).wait_send()
    for desc in moves:
        desc.wait_send()


def solution(mesh):
    n_dp, n_proto = mesh.shape["dp"], mesh.shape["proto"]
    nz = n_dp // 2
    half = nz // 2
    levels = n_dp // GROUP

    def per_device(embeddings, centroids):
        rows, feat = embeddings.shape
        cent = centroids.shape[0]
        own = feat // n_dp
        dma, vmem = pltpu.SemaphoreType.DMA, pltpu.VMEM
        new_centroids, mass = pl.pallas_call(
            functools.partial(kernel, (n_dp, n_proto, rows, feat, cent)),
            out_shape=(jax.ShapeDtypeStruct((own, cent), F32), jax.ShapeDtypeStruct((1, cent), F32)),
            in_specs=[pl.BlockSpec(memory_space=pl.ANY), pl.BlockSpec(memory_space=pltpu.VMEM)],
            out_specs=(pl.BlockSpec(memory_space=pltpu.VMEM), pl.BlockSpec(memory_space=pltpu.VMEM)),
            scratch_shapes=[
                vmem((rows, feat), BF16),
                vmem((feat, rows), BF16),
                vmem((feat, cent), BF16),
                vmem((rows, cent), F32),
                vmem((rows, cent), BF16),
                vmem((feat, cent), F32),
                vmem((1, cent), F32),
                vmem((2, 8, 128), F32),
                vmem((1, cent), F32),
                vmem((SWEEPS, GROUP, 1, cent), F32),
                vmem((SWEEPS, levels, 1, cent), F32),
                vmem((SWEEPS, n_proto, 2, 8, 128), F32),
                vmem((GROUP, 1, 2 * cent), F32),
                vmem((levels, 1, 2 * cent), F32),
                vmem((nz, own, cent), F32),
                vmem((2, 2, half + 1, own, cent // 2), F32),
                dma, dma((1,)),
                dma((2, half)), dma((2, half)), dma((nz,)), dma((nz,)),
                dma((SWEEPS, 2)), dma((SWEEPS, 2)), dma((SWEEPS, 2)),
                dma((2,)), dma((2,)),
                dma((nz,)), dma((nz,)),
                dma((2, 2, half)), dma((2, 2, half)),
            ],
            compiler_params=pltpu.CompilerParams(
                collective_id=0, has_side_effects=True, vmem_limit_bytes=56 * 1024 * 1024),
            cost_estimate=pl.CostEstimate(
                flops=4 * rows * feat * cent, bytes_accessed=2 * rows * feat, transcendentals=rows * cent),
        )(embeddings, centroids)
        return new_centroids, mass.reshape(cent)

    return jax.shard_map(
        per_device,
        mesh=mesh,
        in_specs=(P("dp", None), P("proto", "dp")),
        out_specs=(P("dp", "proto"), P("proto")),
        check_vma=False,
    )
```

time: 576 us -> 153 us (0.27)
  blocking collectives: 300 us -> 0 us
  waiting for transfers between devices: 234 us -> 0 us
  Pallas kernels: 0 us -> 148 us
  other arithmetic: 15.5 us -> 0 us
  between operations: 14.1 us -> 0.64 us
  matrix products: 11.7 us -> 0 us
    psum x7 -> x0, blocking collectives: 300 us -> none  [the longest x3 153 us: per_device(): col_total = lax.psum(jnp.sum(exp_scores * row_scale[:, None], axis=0), 'dp')]
    psum x1 -> x0, waiting for transfers between devices: 162 us -> none  [per_device(): whole_sums = lax.psum(local_sums, 'dp')]
    pallas_call x0 -> x1, Pallas kernels: none -> 148 us  [per_device(): pl.pallas_call(functools.partial(kernel, (n_dp, n_proto, rows, feat, cent...]
    all_gather x1 -> x0, waiting for transfers between devices: 71.5 us -> none  [per_device(): block_piece = lax.all_gather(centroids, 'dp', axis=1, tiled=True)]
    dot_general x2 -> x0, matrix products: 11.7 us -> none  [the longest x1 6.72 us: per_device(): lax.dot_general(unit_rows, weights, (((0,), (0,)), ((), ())), preferred_e...]
    reduce_sum x9 -> x0, other arithmetic: 9.28 us -> none  [the longest x1 3.47 us: per_device(): jnp.sum(values * values, axis=1, keepdims=True) + 1e-06]
  transfers between devices with their start and end apart: 2 -> 0, of which waited for: 2 -> 0; matrix products, arithmetic and copies ran while one was open for 1% -> 0% of each run, Pallas kernels for 0% -> 0%
where the time goes in v1:
time: 153 us
  Pallas kernels  148 us (97%)
  local copies, waits for them, and re-layouts  4.34 us (3%)
    pallas_call x1, Pallas kernels, per_device(): pl.pallas_call(functools.partial(kernel, (n_dp, n_proto, rows, feat, cent...  148 us
    unnamed x3, local copies, waits for them, and re-layouts  4.34 us

profile of v1, /device:TPU:1, one launch (start us, length us, event | category | flops | bytes accessed | tf_op | source)
XLA Modules:
  0.0 152.8 jit_solution(9643925561060807480)
XLA Ops:
  0.6 1.6 %copy.4.cen = bf16[512,48]{1,0:T(8,128)(2,1)} copy(bf16[512,48]{0,1:T(8,128)(2,1)} %param.3) | data formatting | bytes 98304 | tf_op args[1]
  2.2 147.8 %shard_map.41 = (f32[48,512]{1,0:T(8,128)}, f32[1,512]{1,0:T(1,128)}) custom-call(bf16[1536,1536]{1,0:T(8,128)(2,1)} %emb.1, bf16[512,48]{1,0:T(8,128)(2,1)} %copy.4.cen), custom_call_target="tpu_custom_call" | custom-call | flops 4831838208 | bytes 4718592 | tf_op jit(solution)/shard_map/pallas_call | solution.py:311
  150.0 1.5 %copy.7 = f32[48,512]{1,0:T(8,128)} copy(f32[48,512]{1,0:T(8,128)} %get-tuple-element.8) | data formatting | bytes 196608
  151.5 1.2 copy.8

commit v2 on v0

v2 whole, which is shorter than its diff:
```python
import functools

import jax
import jax.numpy as jnp
from jax import lax
from jax.experimental import pallas as pl
from jax.experimental.pallas import tpu as pltpu
from jax.sharding import PartitionSpec as P

SWEEPS = 3
LOGIT_SCALE = 40.0
F32, BF16 = jnp.float32, jnp.bfloat16
MESH = pl.DeviceIdType.MESH
GROUP = 8
SUBS = 3
PARTS = 4
UNIT = 16
LANES = 128


def dot(a, b, dims):
    return lax.dot_general(a, b, (dims, ((), ())), preferred_element_type=F32)


def kernel(sizes, emb, cen, out, mass_out, x, ut, ct, e, w, s, col_a, col_b, row_x,
           fin_a, fin_b, sib, ring, sem_in, g_send, g_recv, gs_send, gs_recv, ca_sem, cb_sem, rx_sem,
           fa_sem, fb_sem, sx_send, sx_recv, r_send, r_recv):
    n_dp, n_proto, rows, feat, cent = sizes
    nz = n_dp // 2
    half = nz // 2
    own = feat // n_dp
    n_rows = rows * n_dp
    n_cent = cent * n_proto
    levels = n_dp // GROUP

    d = lax.axis_index("dp")
    p = lax.axis_index("proto")
    z, c = d // 2, d % 2
    other = d + 1 - 2 * c
    right = ((z + 1) % nz) * 2 + c
    left = ((z + nz - 1) % nz) * 2 + c
    in_group = d % GROUP
    level = d // GROUP
    group_ids = [{"dp": level * GROUP + (in_group + j) % GROUP} for j in range(1, GROUP)]
    level_ids = [{"dp": (d + GROUP * j) % n_dp} for j in range(1, levels)]
    proto_ids = [{"proto": (p + j) % n_proto} for j in range(1, n_proto)]

    barrier = pltpu.get_barrier_semaphore()
    partners = [{"dp": left}, {"dp": right}] + group_ids + level_ids + proto_ids
    for t in partners:
        pl.semaphore_signal(barrier, inc=1, device_id=t, device_id_type=MESH)

    load = pltpu.make_async_copy(emb, x, sem_in)
    load.start()

    def block_rows(o, core):
        return pl.ds(pl.multiple_of((o * 2 + core) * own, own), own)

    ct[block_rows(z, c), :] = cen[...]
    pl.semaphore_wait(barrier, len(partners))

    piece = own // SUBS

    def hop(o, way, step, sub):
        at = ct.at[pl.ds(pl.multiple_of((o * 2 + c) * own + sub * piece, piece), piece)]
        return pltpu.make_async_remote_copy(
            src_ref=at, dst_ref=at, send_sem=g_send.at[way, step, sub], recv_sem=g_recv.at[way, step, sub],
            device_id={"dp": right if way == 0 else left}, device_id_type=MESH)

    def across(o, slot):
        at = ct.at[block_rows(o, c)]
        return pltpu.make_async_remote_copy(
            src_ref=at, dst_ref=at, send_sem=gs_send.at[slot], recv_sem=gs_recv.at[slot],
            device_id={"dp": other}, device_id_type=MESH)

    pending = []

    def launch(desc):
        desc.start()
        pending.append(desc)

    for sub in range(SUBS):
        launch(hop(z, 0, 0, sub))
        launch(hop(z, 1, 0, sub))
    launch(across(z, 0))

    def square(o, core):
        v = ct[block_rows(o, core), :].astype(F32)
        return jnp.sum((v * v).reshape(own // 8, 8, cent), axis=0)

    load.wait()
    tile, short = 256, 128
    eye = (
        lax.broadcasted_iota(jnp.int32, (tile, tile), 0) == lax.broadcasted_iota(jnp.int32, (tile, tile), 1)
    ).astype(BF16)

    def prepare(b):
        at = pl.ds(b * short, short)
        v = x[at, :].astype(F32)
        u = (v * (1.0 / jnp.sqrt(jnp.sum(v * v, axis=1, keepdims=True) + 1e-06))).astype(BF16)
        x[at, :] = u
        for f in range(feat // tile):
            ut[pl.ds(f * tile, tile), at] = dot(
                eye, u[:, f * tile:(f + 1) * tile], ((1,), (1,))).astype(BF16)

    squares = square(z, c)
    behind = [(z, 0)]
    unit = 0
    for step in range(half):
        came = []
        for sub in range(SUBS):
            if unit < rows // short:
                prepare(unit)
                unit += 1
            for way in (0, 1):
                last = half - 1 if way == 0 else half - 2
                if step > last:
                    continue
                o = (z - 1 - step + nz) % nz if way == 0 else (z + 1 + step) % nz
                hop(o, way, step, sub).wait_recv()
                if step < last:
                    launch(hop(o, way, step + 1, sub))
                if sub == SUBS - 1:
                    launch(across(o, 1 + 2 * step + way))
                    came.append((o, 1 + 2 * step + way))
        for o, slot in behind:
            across(o, slot).wait_recv()
            squares = squares + square(o, 1 - c)
        for o, slot in came:
            squares = squares + square(o, c)
        behind = came
    for o, slot in behind:
        across(o, slot).wait_recv()
        squares = squares + square(o, 1 - c)

    scale = LOGIT_SCALE * (1.0 / jnp.sqrt(jnp.sum(squares, axis=0, keepdims=True) + 1e-06))
    m_tile = rows // 4

    def score(b, acc):
        at = pl.ds(pl.multiple_of(b * m_tile, m_tile), m_tile)
        v = jnp.exp(dot(x[at, :], ct[...], ((1,), (0,))) * scale)
        e[at, :] = v
        return acc + jnp.sum(v.reshape(m_tile // 8, 8, cent), axis=0)

    acc = lax.fori_loop(0, 4, score, jnp.zeros((8, cent), F32))

    def exchange(buf, sem, me, ids):
        for t in ids:
            pltpu.make_async_remote_copy(
                src_ref=buf.at[me], dst_ref=buf.at[me], send_sem=sem.at[0], recv_sem=sem.at[1],
                device_id=t, device_id_type=MESH).start()
        whole = buf.at[pl.ds(0, len(ids))]
        done = pltpu.make_async_remote_copy(
            src_ref=whole, dst_ref=whole, send_sem=sem.at[0], recv_sem=sem.at[1],
            device_id=ids[0], device_id_type=MESH)
        pending.append(done)
        done.wait_recv()
        return functools.reduce(lambda a, b: a + b, [buf[k] for k in range(len(ids) + 1)])

    def sum_dp(first, second, first_sem, second_sem):
        second[level] = exchange(first, first_sem, in_group, group_ids)
        return exchange(second, second_sem, level, level_ids)

    lane = lax.broadcasted_iota(jnp.int32, (8, LANES), 1)
    tiles = [(0, LANES), (LANES, rows // 8)]

    for i in range(SWEEPS):
        col_a[i, in_group] = jnp.sum(acc, axis=0, keepdims=True)
        cv = 1.0 / (n_cent * sum_dp(col_a.at[i], col_b.at[i], ca_sem.at[i], cb_sem.at[i]))
        cb = jnp.broadcast_to(cv, (8, cent))

        totals = []
        for lo, hi in tiles:
            def row_step(g, t):
                for k in range(UNIT):
                    q = e[pl.ds(pl.multiple_of((lo + g * UNIT + k) * 8, 8), 8), :] * cb
                    q = functools.reduce(
                        lambda a, b: a + b, [q[:, m * LANES:(m + 1) * LANES] for m in range(cent // LANES)])
                    t = jnp.where(lane == g * UNIT + k, jnp.sum(q, axis=1, keepdims=True), t)
                return t

            totals.append(lax.fori_loop(0, (hi - lo) // UNIT, row_step, jnp.zeros((8, LANES), F32)))
        row_x[i, p, 0] = totals[0][0:4]
        row_x[i, p, 1] = totals[0][4:8]
        row_x[i, p, 2] = totals[1][0:4] + pltpu.roll(totals[1], LANES // 2, 1)[4:8]
        rv = 1.0 / (n_rows * exchange(row_x.at[i], rx_sem.at[i], p, proto_ids))
        r0 = jnp.concatenate([rv[0], rv[1]], axis=0)
        r1 = jnp.concatenate([rv[2], pltpu.roll(rv[2], LANES // 2, 1)], axis=0)

        final = i == SWEEPS - 1
        nc = jnp.broadcast_to(n_rows * cv, (8, cent))
        acc = jnp.zeros((8, cent), F32)
        for (lo, hi), r in zip(tiles, (r0, r1)):
            def col_step(g, st):
                a, r = st
                for k in range(0, UNIT, 2):
                    at = pl.multiple_of((lo + g * UNIT + k) * 8, 16)
                    pair = [e[pl.ds(at + 8 * m, 8), :] * jnp.broadcast_to(r[:, k + m:k + m + 1], (8, cent))
                            for m in range(2)]
                    a = a + pair[0] + pair[1]
                    if final:
                        w[pl.ds(at, 16), :] = jnp.concatenate([v * nc for v in pair], axis=0).astype(BF16)
                return a, pltpu.roll(r, LANES - UNIT, 1)

            acc, _ = lax.fori_loop(0, (hi - lo) // UNIT, col_step, (acc, r))

    def swap(rel):
        return pltpu.make_async_remote_copy(
            src_ref=s.at[rel, pl.ds(pl.multiple_of((1 - c) * own, own), own)], dst_ref=sib.at[rel],
            send_sem=sx_send.at[rel], recv_sem=sx_recv.at[rel],
            device_id={"dp": other}, device_id_type=MESH)

    def make_sums(rels):
        u = [ut[pl.ds(pl.multiple_of(((z + rel) % nz) * 2 * own, 2 * own), 2 * own), :] for rel in rels]
        v = dot(jnp.concatenate(u, axis=0) if len(u) > 1 else u[0], w[...], ((1,), (0,)))
        for k, rel in enumerate(rels):
            s[rel] = v[k * 2 * own:(k + 1) * 2 * own]
            launch(swap(rel))

    wide = cent // PARTS
    flows = []
    for hops in (half, half - 1):
        for m in range(PARTS // 2):
            for way in (0, 1):
                first = way == (0 if hops == half else 1)
                flows.append((way, m if first else PARTS // 2 + m, hops))

    def link(way, part, t):
        return pltpu.make_async_remote_copy(
            src_ref=ring.at[way, part, t], dst_ref=ring.at[way, part, t + 1],
            send_sem=r_send.at[way, part, t], recv_sem=r_recv.at[way, part, t],
            device_id={"dp": right if way == 0 else left}, device_id_type=MESH)

    own_rows = pl.ds(pl.multiple_of(c * own, own), own)

    def pair_sum(rel, part):
        cols = pl.ds(part * wide, wide)
        return s[rel, own_rows, cols] + sib[rel, :, cols]

    orders = [[half]] + [[half - q, half + q] for q in range(1, half)] + [[0]]
    for k in range(3):
        make_sums(orders[k])
    ready = set()
    for t in range(half):
        for way, part, hops in flows:
            if t >= hops:
                continue
            rel = hops - t if way == 0 else nz - (hops - t)
            if rel not in ready:
                swap(rel).wait_recv()
                ready.add(rel)
            v = pair_sum(rel, part)
            if t > 0:
                link(way, part, t - 1).wait_recv()
                v = v + ring[way, part, t]
            ring[way, part, t] = v
            launch(link(way, part, t))
        if t + 3 < len(orders):
            make_sums(orders[t + 3])
    swap(0).wait_recv()
    for way, part, hops in flows:
        link(way, part, hops - 1).wait_recv()
    parts = []
    for part in range(PARTS):
        v = pair_sum(0, part)
        for way, q, hops in flows:
            if q == part:
                v = v + ring[way, q, hops]
        parts.append(v)
    sums = jnp.concatenate(parts, axis=1)

    fin_a[in_group, :, 0:cent] = jnp.sum(acc, axis=0, keepdims=True)
    fin_a[in_group, :, cent:2 * cent] = jnp.sum(sums * sums, axis=0, keepdims=True)
    tot = sum_dp(fin_a, fin_b, fa_sem, fb_sem)
    mass_out[...] = n_cent * cv * tot[:, 0:cent]
    out[...] = sums * (1.0 / jnp.sqrt(tot[:, cent:2 * cent] + 1e-06))

    for desc in pending:
        desc.wait_send()


def hand_over(sums, mass, sums_out, mass_out):
    sums_out[...] = sums[...]
    mass_out[...] = mass[...]


def solution(mesh):
    n_dp, n_proto = mesh.shape["dp"], mesh.shape["proto"]
    nz = n_dp // 2
    half = nz // 2
    levels = n_dp // GROUP

    def per_device(embeddings, centroids):
        rows, feat = embeddings.shape
        cent = centroids.shape[0]
        own = feat // n_dp
        dma, vmem = pltpu.SemaphoreType.DMA, pltpu.VMEM
        whole = pl.BlockSpec(memory_space=pltpu.VMEM)
        shapes = (jax.ShapeDtypeStruct((own, cent), F32), jax.ShapeDtypeStruct((1, cent), F32))
        sums, mass = pl.pallas_call(
            functools.partial(kernel, (n_dp, n_proto, rows, feat, cent)),
            out_shape=shapes,
            in_specs=[pl.BlockSpec(memory_space=pl.ANY), whole],
            out_specs=(whole, whole),
            scratch_shapes=[
                vmem((rows, feat), BF16),
                vmem((feat, rows), BF16),
                vmem((feat, cent), BF16),
                vmem((rows, cent), F32),
                vmem((rows, cent), BF16),
                vmem((nz, 2 * own, cent), F32),
                vmem((SWEEPS, GROUP, 1, cent), F32),
                vmem((SWEEPS, levels, 1, cent), F32),
                vmem((SWEEPS, n_proto, 3, 4, LANES), F32),
                vmem((GROUP, 1, 2 * cent), F32),
                vmem((levels, 1, 2 * cent), F32),
                vmem((nz, own, cent), F32),
                vmem((2, PARTS, half + 1, own, cent // PARTS), F32),
                dma,
                dma((2, half, SUBS)), dma((2, half, SUBS)), dma((nz,)), dma((nz,)),
                dma((SWEEPS, 2)), dma((SWEEPS, 2)), dma((SWEEPS, 2)),
                dma((2,)), dma((2,)),
                dma((nz,)), dma((nz,)),
                dma((2, PARTS, half)), dma((2, PARTS, half)),
            ],
            compiler_params=pltpu.CompilerParams(
                collective_id=0, has_side_effects=True, vmem_limit_bytes=56 * 1024 * 1024),
            cost_estimate=pl.CostEstimate(
                flops=4 * rows * feat * cent, bytes_accessed=2 * rows * feat, transcendentals=rows * cent),
        )(embeddings, centroids.T)
        new_centroids, mass = pl.pallas_call(
            hand_over, out_shape=shapes, in_specs=[whole, whole], out_specs=(whole, whole))(sums, mass)
        return new_centroids, mass.reshape(cent)

    return jax.shard_map(
        per_device,
        mesh=mesh,
        in_specs=(P("dp", None), P("proto", "dp")),
        out_specs=(P("dp", "proto"), P("proto")),
        check_vma=False,
    )
```

time: 576 us -> 146 us (0.25)
  blocking collectives: 300 us -> 0 us
  waiting for transfers between devices: 234 us -> 0 us
  Pallas kernels: 0 us -> 145 us
  other arithmetic: 15.5 us -> 0 us
  between operations: 14.1 us -> 0.64 us
  matrix products: 11.7 us -> 0 us
    psum x7 -> x0, blocking collectives: 300 us -> none  [the longest x3 153 us: per_device(): col_total = lax.psum(jnp.sum(exp_scores * row_scale[:, None], axis=0), 'dp')]
    psum x1 -> x0, waiting for transfers between devices: 162 us -> none  [per_device(): whole_sums = lax.psum(local_sums, 'dp')]
    pallas_call x0 -> x2, Pallas kernels: none -> 145 us  [the longest x1 144 us: per_device(): pl.pallas_call(functools.partial(kernel, (n_dp, n_proto, rows, feat, cent...]
    all_gather x1 -> x0, waiting for transfers between devices: 71.5 us -> none  [per_device(): block_piece = lax.all_gather(centroids, 'dp', axis=1, tiled=True)]
    dot_general x2 -> x0, matrix products: 11.7 us -> none  [the longest x1 6.72 us: per_device(): lax.dot_general(unit_rows, weights, (((0,), (0,)), ((), ())), preferred_e...]
    reduce_sum x9 -> x0, other arithmetic: 9.28 us -> none  [the longest x1 3.47 us: per_device(): jnp.sum(values * values, axis=1, keepdims=True) + 1e-06]
  transfers between devices with their start and end apart: 2 -> 0, of which waited for: 2 -> 0; matrix products, arithmetic and copies ran while one was open for 1% -> 0% of each run, Pallas kernels for 0% -> 0%
where the time goes in v2:
time: 146 us
  Pallas kernels  145 us (99%)
    pallas_call x1, Pallas kernels, per_device(): pl.pallas_call(functools.partial(kernel, (n_dp, n_proto, rows, feat, cent...  144 us

profile of v2, /device:TPU:1, one launch (start us, length us, event | category | flops | bytes accessed | tf_op | source)
XLA Modules:
  0.0 145.8 jit_solution(12468043898270752107)
XLA Ops:
  0.6 143.6 %shard_map.41 = (f32[48,512]{1,0:T(8,128)}, f32[1,512]{1,0:T(1,128)}) custom-call(bf16[1536,1536]{1,0:T(8,128)(2,1)} %emb.1, bf16[48,512]{1,0:T(8,128)(2,1)} %bitcast.2), custom_call_target="tpu_custom_call" | custom-call | flops 4831838208 | bytes 4718592 | tf_op jit(solution)/shard_map/pallas_call | solution.py:300
  144.3 1.5 %shard_map.42 = (f32[48,512]{1,0:T(8,128)}, f32[1,512]{1,0:T(1,128)}) custom-call(f32[48,512]{1,0:T(8,128)} %get-tuple-element.6.sums, f32[1,512]{1,0:T(1,128)} %get-tuple-element.7.mass), custom_call_target="tpu_custom_call" | custom-call | tf_op jit(solution)/shard_map/pallas_call | solution.py:331

commit v3 on v2

v3 whole, which is shorter than its diff:
```python
import functools

import jax
import jax.numpy as jnp
from jax import lax
from jax.experimental import pallas as pl
from jax.experimental.pallas import tpu as pltpu
from jax.sharding import PartitionSpec as P

SWEEPS = 3
LOGIT_SCALE = 40.0
F32, BF16 = jnp.float32, jnp.bfloat16
MESH = pl.DeviceIdType.MESH
GROUP = 8
SUBS = 3
PARTS = 4
UNIT = 16
LANES = 128


def dot(a, b, dims):
    return lax.dot_general(a, b, (dims, ((), ())), preferred_element_type=F32)


def kernel(sizes, emb, cen, out, mass_out, x, ut, ct, e, w, s, acc, cvec, rvec, col_a, col_b, row_x,
           fin_a, fin_b, sib, ring, sem_in, g_send, g_recv, gs_recv, c_sem, rx_sem, f_sem,
           sx_send, sx_recv, r_send, r_recv):
    n_dp, n_proto, rows, feat, cent = sizes
    nz = n_dp // 2
    half = nz // 2
    own = feat // n_dp
    n_rows = rows * n_dp
    n_cent = cent * n_proto
    levels = n_dp // GROUP

    d = lax.axis_index("dp")
    p = lax.axis_index("proto")
    z, c = d // 2, d % 2
    other = d + 1 - 2 * c
    right = ((z + 1) % nz) * 2 + c
    left = ((z + nz - 1) % nz) * 2 + c
    in_group = d % GROUP
    level = d // GROUP
    group_ids = [{"dp": level * GROUP + (in_group + j) % GROUP} for j in range(1, GROUP)]
    level_ids = [{"dp": (d + GROUP * j) % n_dp} for j in range(1, levels)]
    proto_ids = [{"proto": (p + j) % n_proto} for j in range(1, n_proto)]

    barrier = pltpu.get_barrier_semaphore()
    partners = [{"dp": left}, {"dp": right}] + group_ids + level_ids + proto_ids
    for t in partners:
        pl.semaphore_signal(barrier, inc=1, device_id=t, device_id_type=MESH)

    load = pltpu.make_async_copy(emb, x, sem_in)
    load.start()

    def block_rows(o, core):
        return pl.ds(pl.multiple_of((o * 2 + core) * own, own), own)

    ct[block_rows(z, c), :] = cen[...]
    pl.semaphore_wait(barrier, len(partners))

    piece = own // SUBS

    def hop(o, way, step, sub):
        at = ct.at[pl.ds(pl.multiple_of((o * 2 + c) * own + sub * piece, piece), piece)]
        return pltpu.make_async_remote_copy(
            src_ref=at, dst_ref=at, send_sem=g_send, recv_sem=g_recv.at[way, step, sub],
            device_id={"dp": right if way == 0 else left}, device_id_type=MESH)

    def across(o, slot):
        at = ct.at[block_rows(o, c)]
        return pltpu.make_async_remote_copy(
            src_ref=at, dst_ref=at, send_sem=g_send, recv_sem=gs_recv.at[slot],
            device_id={"dp": other}, device_id_type=MESH)

    def square(o, core):
        v = ct[block_rows(o, core), :].astype(F32)
        acc[...] += jnp.sum((v * v).reshape(own // 8, 8, cent), axis=0)

    def start(step, sub):
        hop(z, 0, 0, sub).start()
        hop(z, 1, 0, sub).start()
        return step

    lax.fori_loop(0, SUBS, lambda sub, carry: start(carry, sub), 0)
    across(z, 0).start()

    acc[...] = jnp.zeros((8, cent), F32)
    square(z, c)
    load.wait()
    tile, short, thin = 256, 128, 32
    eye = (
        lax.broadcasted_iota(jnp.int32, (tile, tile), 0) == lax.broadcasted_iota(jnp.int32, (tile, tile), 1)
    ).astype(BF16)

    def prepare(b):
        def norm(k, carry):
            at = pl.ds(pl.multiple_of(b * short + k * thin, thin), thin)
            v = x[at, :].astype(F32)
            x[at, :] = (v * (1.0 / jnp.sqrt(jnp.sum(v * v, axis=1, keepdims=True) + 1e-06))).astype(BF16)
            return carry

        lax.fori_loop(0, short // thin, norm, 0)
        at = pl.ds(pl.multiple_of(b * short, short), short)

        def turn(f, carry):
            cols = pl.ds(pl.multiple_of(f * tile, tile), tile)
            ut[cols, at] = dot(eye, x[at, cols], ((1,), (1,))).astype(BF16)
            return carry

        lax.fori_loop(0, feat // tile, turn, 0)

    def gather_step(step, carry):
        o_right = (z - 1 - step + nz) % nz
        o_left = (z + 1 + step) % nz

        def gather_piece(sub, carry):
            unit = step * SUBS + sub

            @pl.when(unit < rows // short)
            def _():
                prepare(unit)

            hop(o_right, 0, step, sub).wait_recv()

            @pl.when(step < half - 1)
            def _():
                hop(o_right, 0, step + 1, sub).start()
                hop(o_left, 1, step, sub).wait_recv()

            @pl.when(step < half - 2)
            def _():
                hop(o_left, 1, step + 1, sub).start()

            return carry

        lax.fori_loop(0, SUBS, gather_piece, 0)
        across(o_right, 1 + 2 * step).start()
        square(o_right, c)

        @pl.when(step < half - 1)
        def _():
            across(o_left, 2 + 2 * step).start()
            square(o_left, c)

        @pl.when(step == 0)
        def _():
            across(z, 0).wait_recv()
            square(z, 1 - c)

        @pl.when(step > 0)
        def _():
            across(o_right, 2 * step - 1).wait_recv()
            across(o_left, 2 * step).wait_recv()
            square((o_right + 1) % nz, 1 - c)
            square((o_left + nz - 1) % nz, 1 - c)

        return carry

    lax.fori_loop(0, half, gather_step, 0)
    across(z, nz - 1).wait_recv()
    square((z + half) % nz, 1 - c)

    scale = LOGIT_SCALE * (1.0 / jnp.sqrt(jnp.sum(acc[...], axis=0, keepdims=True) + 1e-06))
    m_tile = rows // 4

    def score(b, total):
        at = pl.ds(pl.multiple_of(b * m_tile, m_tile), m_tile)
        v = jnp.exp(dot(x[at, :], ct[...], ((1,), (0,))) * scale)
        e[at, :] = v
        return total + jnp.sum(v.reshape(m_tile // 8, 8, cent), axis=0)

    acc[...] = lax.fori_loop(0, 4, score, jnp.zeros((8, cent), F32))

    def exchange(buf, send, recv, me, ids):
        for t in ids:
            pltpu.make_async_remote_copy(
                src_ref=buf.at[me], dst_ref=buf.at[me], send_sem=send, recv_sem=recv,
                device_id=t, device_id_type=MESH).start()
        whole = buf.at[pl.ds(0, len(ids))]
        done = pltpu.make_async_remote_copy(
            src_ref=whole, dst_ref=whole, send_sem=send, recv_sem=recv,
            device_id=ids[0], device_id_type=MESH)
        done.wait_recv()
        return functools.reduce(lambda a, b: a + b, [buf[k] for k in range(len(ids) + 1)]), done

    def sum_dp(first, second, sem):
        second[level], sent_first = exchange(first, sem.at[0], sem.at[1], in_group, group_ids)
        result, sent_second = exchange(second, sem.at[2], sem.at[3], level, level_ids)
        return result, (sent_first, sent_second)

    lane = lax.broadcasted_iota(jnp.int32, (8, LANES), 1)
    tiles = [(0, LANES), (LANES, rows // 8)]

    def column_pass(scaled):
        total = jnp.zeros((8, cent), F32)
        for m, (lo, hi) in enumerate(tiles):
            def col_step(g, st):
                a, r = st
                for k in range(0, UNIT, 2):
                    at = pl.multiple_of((lo + g * UNIT + k) * 8, 16)
                    pair = [e[pl.ds(at + 8 * m, 8), :] * jnp.broadcast_to(r[:, k + m:k + m + 1], (8, cent))
                            for m in range(2)]
                    a = a + pair[0] + pair[1]
                    if scaled is not None:
                        w[pl.ds(at, 16), :] = jnp.concatenate([v * scaled for v in pair], axis=0).astype(BF16)
                return a, pltpu.roll(r, LANES - UNIT, 1)

            total, _ = lax.fori_loop(0, (hi - lo) // UNIT, col_step, (total, rvec[m]))
        acc[...] = total

    def sweep(i, carry):
        col_a[i, in_group] = jnp.sum(acc[...], axis=0, keepdims=True)
        col_total, sent = sum_dp(col_a.at[i], col_b.at[i], c_sem.at[i])
        cv = 1.0 / (n_cent * col_total)
        cvec[...] = cv
        cb = jnp.broadcast_to(cv, (8, cent))

        totals = []
        for lo, hi in tiles:
            def row_step(g, t):
                for k in range(UNIT):
                    q = e[pl.ds(pl.multiple_of((lo + g * UNIT + k) * 8, 8), 8), :] * cb
                    q = functools.reduce(
                        lambda a, b: a + b, [q[:, m * LANES:(m + 1) * LANES] for m in range(cent // LANES)])
                    t = jnp.where(lane == g * UNIT + k, jnp.sum(q, axis=1, keepdims=True), t)
                return t

            totals.append(lax.fori_loop(0, (hi - lo) // UNIT, row_step, jnp.zeros((8, LANES), F32)))
        row_x[i, p, 0] = totals[0][0:4]
        row_x[i, p, 1] = totals[0][4:8]
        row_x[i, p, 2] = totals[1][0:4] + pltpu.roll(totals[1], LANES // 2, 1)[4:8]
        row_total, sent_row = exchange(row_x.at[i], rx_sem.at[i, 0], rx_sem.at[i, 1], p, proto_ids)
        rv = 1.0 / (n_rows * row_total)
        rvec[0] = jnp.concatenate([rv[0], rv[1]], axis=0)
        rvec[1] = jnp.concatenate([rv[2], pltpu.roll(rv[2], LANES // 2, 1)], axis=0)

        @pl.when(i < SWEEPS - 1)
        def _():
            column_pass(None)

        for desc in sent + (sent_row,):
            desc.wait_send()
        return carry

    lax.fori_loop(0, SWEEPS, sweep, 0)
    column_pass(jnp.broadcast_to(n_rows * cvec[...], (8, cent)))

    def swap(rel):
        return pltpu.make_async_remote_copy(
            src_ref=s.at[rel, pl.ds(pl.multiple_of((1 - c) * own, own), own)], dst_ref=sib.at[rel],
            send_sem=sx_send, recv_sem=sx_recv.at[rel],
            device_id={"dp": other}, device_id_type=MESH)

    def make_sums(q):
        rels = (half - q, lax.select(q == 0, 0, half + q))
        u = [ut[pl.ds(pl.multiple_of(((z + rel) % nz) * 2 * own, 2 * own), 2 * own), :] for rel in rels]
        v = dot(jnp.concatenate(u, axis=0), w[...], ((1,), (0,)))
        for k, rel in enumerate(rels):
            s[rel] = v[k * 2 * own:(k + 1) * 2 * own]
            swap(rel).start()

    wide = cent // PARTS
    flows = []
    for hops in (half, half - 1):
        for m in range(PARTS // 2):
            for way in (0, 1):
                first = way == (0 if hops == half else 1)
                flows.append((way, m if first else PARTS // 2 + m, hops))

    def link(way, part, t):
        return pltpu.make_async_remote_copy(
            src_ref=ring.at[way, part, t], dst_ref=ring.at[way, part, t + 1],
            send_sem=r_send, recv_sem=r_recv.at[way, part, t],
            device_id={"dp": right if way == 0 else left}, device_id_type=MESH)

    own_rows = pl.ds(pl.multiple_of(c * own, own), own)

    def pair_sum(rel, part):
        cols = pl.ds(part * wide, wide)
        return s[rel, own_rows, cols] + sib[rel, :, cols]

    def flow(way, part, hops, t):
        rel = hops - t if way == 0 else nz - hops + t

        @pl.when(t == 0)
        def _():
            ring[way, part, 0] = pair_sum(rel, part)

        @pl.when(t > 0)
        def _():
            link(way, part, t - 1).wait_recv()
            ring[way, part, t] = pair_sum(rel, part) + ring[way, part, t]

        link(way, part, t).start()

    ahead = 3

    def ring_step(k, carry):
        t = k - ahead

        @pl.when(t == 0)
        def _():
            swap(half).wait_recv()

        @pl.when(t >= 0)
        def _():
            for way, part, hops in flows:
                if hops == half:
                    flow(way, part, hops, t)

        @pl.when((t >= 0) & (t < half - 1))
        def _():
            swap(half - 1 - t).wait_recv()
            swap(half + 1 + t).wait_recv()
            for way, part, hops in flows:
                if hops < half:
                    flow(way, part, hops, t)

        @pl.when(k < half)
        def _():
            make_sums(k)

        return carry

    lax.fori_loop(0, half + ahead, ring_step, 0)
    swap(0).wait_recv()
    for way, part, hops in flows:
        link(way, part, hops - 1).wait_recv()
    parts = []
    for part in range(PARTS):
        v = pair_sum(0, part)
        for way, q, hops in flows:
            if q == part:
                v = v + ring[way, q, hops]
        parts.append(v)
    sums = jnp.concatenate(parts, axis=1)

    fin_a[in_group, :, 0:cent] = jnp.sum(acc[...], axis=0, keepdims=True)
    fin_a[in_group, :, cent:2 * cent] = jnp.sum(sums * sums, axis=0, keepdims=True)
    tot, sent = sum_dp(fin_a, fin_b, f_sem)
    mass_out[...] = n_cent * cvec[...] * tot[:, 0:cent]
    out[...] = sums * (1.0 / jnp.sqrt(tot[:, cent:2 * cent] + 1e-06))

    for desc in sent:
        desc.wait_send()
    for ref, sem in ((ct.at[pl.ds(0, (2 * nz - 1) * own)], g_send), (sib, sx_send), (sib.at[pl.ds(0, nz - 1)], r_send)):
        pltpu.make_async_remote_copy(
            src_ref=ref, dst_ref=ref, send_sem=sem, recv_sem=sem,
            device_id={"dp": other}, device_id_type=MESH).wait_send()


def hand_over(sums, mass, sums_out, mass_out):
    sums_out[...] = sums[...]
    mass_out[...] = mass[...]


def solution(mesh):
    n_dp, n_proto = mesh.shape["dp"], mesh.shape["proto"]
    nz = n_dp // 2
    half = nz // 2
    levels = n_dp // GROUP

    def per_device(embeddings, centroids):
        rows, feat = embeddings.shape
        cent = centroids.shape[0]
        own = feat // n_dp
        dma, vmem = pltpu.SemaphoreType.DMA, pltpu.VMEM
        whole = pl.BlockSpec(memory_space=pltpu.VMEM)
        shapes = (jax.ShapeDtypeStruct((own, cent), F32), jax.ShapeDtypeStruct((1, cent), F32))
        sums, mass = pl.pallas_call(
            functools.partial(kernel, (n_dp, n_proto, rows, feat, cent)),
            out_shape=shapes,
            in_specs=[pl.BlockSpec(memory_space=pl.ANY), whole],
            out_specs=(whole, whole),
            scratch_shapes=[
                vmem((rows, feat), BF16),
                vmem((feat, rows), BF16),
                vmem((feat, cent), BF16),
                vmem((rows, cent), F32),
                vmem((rows, cent), BF16),
                vmem((nz, 2 * own, cent), F32),
                vmem((8, cent), F32),
                vmem((1, cent), F32),
                vmem((2, 8, LANES), F32),
                vmem((SWEEPS, GROUP, 1, cent), F32),
                vmem((SWEEPS, levels, 1, cent), F32),
                vmem((SWEEPS, n_proto, 3, 4, LANES), F32),
                vmem((GROUP, 1, 2 * cent), F32),
                vmem((levels, 1, 2 * cent), F32),
                vmem((nz, own, cent), F32),
                vmem((2, PARTS, half + 1, own, cent // PARTS), F32),
                dma, dma, dma((2, half, SUBS)), dma((nz,)),
                dma((SWEEPS, 4)), dma((SWEEPS, 2)), dma((4,)),
                dma, dma((nz,)), dma, dma((2, PARTS, half)),
            ],
            compiler_params=pltpu.CompilerParams(
                collective_id=0, has_side_effects=True, vmem_limit_bytes=56 * 1024 * 1024),
            cost_estimate=pl.CostEstimate(
                flops=4 * rows * feat * cent, bytes_accessed=2 * rows * feat, transcendentals=rows * cent),
        )(embeddings, centroids.T)
        new_centroids, mass = pl.pallas_call(
            hand_over, out_shape=shapes, in_specs=[whole, whole], out_specs=(whole, whole))(sums, mass)
        return new_centroids, mass.reshape(cent)

    return jax.shard_map(
        per_device,
        mesh=mesh,
        in_specs=(P("dp", None), P("proto", "dp")),
        out_specs=(P("dp", "proto"), P("proto")),
        check_vma=False,
    )
```

time: 146 us -> 152 us (1.041)
  Pallas kernels: 145 us -> 151 us
    pallas_call x1, Pallas kernels: 144 us -> 149 us  [per_device(): pl.pallas_call(functools.partial(kernel, (n_dp, n_proto, rows, feat, cent...]
where the time goes in v3:
time: 152 us; the launch traced here: 151 us
  Pallas kernels  151 us (99%)
    pallas_call x1, Pallas kernels, per_device(): pl.pallas_call(functools.partial(kernel, (n_dp, n_proto, rows, feat, cent...  149 us

profile of v3, /device:TPU:1, one launch (start us, length us, event | category | flops | bytes accessed | tf_op | source)
XLA Modules:
  0.0 151.4 jit_solution(8815661962950833537)
XLA Ops:
  0.6 149.2 %shard_map.41 = (f32[48,512]{1,0:T(8,128)}, f32[1,512]{1,0:T(1,128)}) custom-call(bf16[1536,1536]{1,0:T(8,128)(2,1)} %emb.1, bf16[48,512]{1,0:T(8,128)(2,1)} %bitcast.2), custom_call_target="tpu_custom_call" | custom-call | flops 4831838208 | bytes 4718592 | tf_op jit(solution)/shard_map/pallas_call | solution.py:371
  149.9 1.5 %shard_map.42 = (f32[48,512]{1,0:T(8,128)}, f32[1,512]{1,0:T(1,128)}) custom-call(f32[48,512]{1,0:T(8,128)} %get-tuple-element.6.sums, f32[1,512]{1,0:T(1,128)} %get-tuple-element.7.mass), custom_call_target="tpu_custom_call" | custom-call | tf_op jit(solution)/shard_map/pallas_call | solution.py:402

commit v4 on v2

--- a/solution.py
+++ b/solution.py
@@ -14,7 +14,7 @@
 GROUP = 8
 SUBS = 3
 PARTS = 4
-UNIT = 16
+UNIT = 32
 LANES = 128
 
 
@@ -22,8 +22,8 @@
     return lax.dot_general(a, b, (dims, ((), ())), preferred_element_type=F32)
 
 
-def kernel(sizes, emb, cen, out, mass_out, x, ut, ct, e, w, s, col_a, col_b, row_x,
-           fin_a, fin_b, sib, ring, sem_in, g_send, g_recv, gs_send, gs_recv, ca_sem, cb_sem, rx_sem,
+def kernel(sizes, emb, cen, out, mass_out, x, ut, ct, e, w, s, col_a, col_b, row_x, row_y,
+           fin_a, fin_b, sib, ring, sem_in, g_send, g_recv, gs_send, gs_recv, ca_sem, cb_sem, rx_sem, ry_sem,
            fa_sem, fb_sem, sx_send, sx_recv, r_send, r_recv):
     n_dp, n_proto, rows, feat, cent = sizes
     nz = n_dp // 2
@@ -32,6 +32,7 @@
     n_rows = rows * n_dp
     n_cent = cent * n_proto
     levels = n_dp // GROUP
+    side = int(n_proto**0.5)
 
     d = lax.axis_index("dp")
     p = lax.axis_index("proto")
@@ -43,10 +44,12 @@
     level = d // GROUP
     group_ids = [{"dp": level * GROUP + (in_group + j) % GROUP} for j in range(1, GROUP)]
     level_ids = [{"dp": (d + GROUP * j) % n_dp} for j in range(1, levels)]
-    proto_ids = [{"proto": (p + j) % n_proto} for j in range(1, n_proto)]
+    px, py = p // side, p % side
+    x_ids = [{"proto": (p + side * j) % n_proto} for j in range(1, side)]
+    y_ids = [{"proto": px * side + (py + j) % side} for j in range(1, side)]
 
     barrier = pltpu.get_barrier_semaphore()
-    partners = [{"dp": left}, {"dp": right}] + group_ids + level_ids + proto_ids
+    partners = [{"dp": left}, {"dp": right}] + group_ids + level_ids + x_ids + y_ids
     for t in partners:
         pl.semaphore_signal(barrier, inc=1, device_id=t, device_id_type=MESH)
 
@@ -99,9 +102,12 @@
         v = x[at, :].astype(F32)
         u = (v * (1.0 / jnp.sqrt(jnp.sum(v * v, axis=1, keepdims=True) + 1e-06))).astype(BF16)
         x[at, :] = u
+
+    def turn(b):
+        at = pl.ds(b * short, short)
         for f in range(feat // tile):
             ut[pl.ds(f * tile, tile), at] = dot(
-                eye, u[:, f * tile:(f + 1) * tile], ((1,), (1,))).astype(BF16)
+                eye, x[at, f * tile:(f + 1) * tile], ((1,), (1,))).astype(BF16)
 
     squares = square(z, c)
     behind = [(z, 0)]
@@ -144,7 +150,7 @@
 
     acc = lax.fori_loop(0, 4, score, jnp.zeros((8, cent), F32))
 
-    def exchange(buf, sem, me, ids):
+    def exchange(buf, sem, me, ids, units=()):
         for t in ids:
             pltpu.make_async_remote_copy(
                 src_ref=buf.at[me], dst_ref=buf.at[me], send_sem=sem.at[0], recv_sem=sem.at[1],
@@ -154,19 +160,24 @@
             src_ref=whole, dst_ref=whole, send_sem=sem.at[0], recv_sem=sem.at[1],
             device_id=ids[0], device_id_type=MESH)
         pending.append(done)
+        for b in units:
+            turn(b)
         done.wait_recv()
         return functools.reduce(lambda a, b: a + b, [buf[k] for k in range(len(ids) + 1)])
 
-    def sum_dp(first, second, first_sem, second_sem):
-        second[level] = exchange(first, first_sem, in_group, group_ids)
-        return exchange(second, second_sem, level, level_ids)
+    def sum_dp(first, second, first_sem, second_sem, units=((), ())):
+        second[level] = exchange(first, first_sem, in_group, group_ids, units[0])
+        return exchange(second, second_sem, level, level_ids, units[1])
 
     lane = lax.broadcasted_iota(jnp.int32, (8, LANES), 1)
     tiles = [(0, LANES), (LANES, rows // 8)]
 
+    per_sweep = rows // short // SWEEPS
     for i in range(SWEEPS):
+        turns = range(i * per_sweep, (i + 1) * per_sweep)
         col_a[i, in_group] = jnp.sum(acc, axis=0, keepdims=True)
-        cv = 1.0 / (n_cent * sum_dp(col_a.at[i], col_b.at[i], ca_sem.at[i], cb_sem.at[i]))
+        cv = 1.0 / (n_cent * sum_dp(
+            col_a.at[i], col_b.at[i], ca_sem.at[i], cb_sem.at[i], (turns[0:1], turns[1:2])))
         cb = jnp.broadcast_to(cv, (8, cent))
 
         totals = []
@@ -180,10 +191,11 @@
                 return t
 
             totals.append(lax.fori_loop(0, (hi - lo) // UNIT, row_step, jnp.zeros((8, LANES), F32)))
-        row_x[i, p, 0] = totals[0][0:4]
-        row_x[i, p, 1] = totals[0][4:8]
-        row_x[i, p, 2] = totals[1][0:4] + pltpu.roll(totals[1], LANES // 2, 1)[4:8]
-        rv = 1.0 / (n_rows * exchange(row_x.at[i], rx_sem.at[i], p, proto_ids))
+        row_x[i, px, 0] = totals[0][0:4]
+        row_x[i, px, 1] = totals[0][4:8]
+        row_x[i, px, 2] = totals[1][0:4] + pltpu.roll(totals[1], LANES // 2, 1)[4:8]
+        row_y[i, py] = exchange(row_x.at[i], rx_sem.at[i], px, x_ids, turns[2:3])
+        rv = 1.0 / (n_rows * exchange(row_y.at[i], ry_sem.at[i], py, y_ids, turns[3:]))
         r0 = jnp.concatenate([rv[0], rv[1]], axis=0)
         r1 = jnp.concatenate([rv[2], pltpu.roll(rv[2], LANES // 2, 1)], axis=0)
 
@@ -289,6 +301,7 @@
     nz = n_dp // 2
     half = nz // 2
     levels = n_dp // GROUP
+    side = int(n_proto**0.5)
 
     def per_device(embeddings, centroids):
         rows, feat = embeddings.shape
@@ -311,14 +324,15 @@
                 vmem((nz, 2 * own, cent), F32),
                 vmem((SWEEPS, GROUP, 1, cent), F32),
                 vmem((SWEEPS, levels, 1, cent), F32),
-                vmem((SWEEPS, n_proto, 3, 4, LANES), F32),
+                vmem((SWEEPS, side, 3, 4, LANES), F32),
+                vmem((SWEEPS, side, 3, 4, LANES), F32),
                 vmem((GROUP, 1, 2 * cent), F32),
                 vmem((levels, 1, 2 * cent), F32),
                 vmem((nz, own, cent), F32),
                 vmem((2, PARTS, half + 1, own, cent // PARTS), F32),
                 dma,
                 dma((2, half, SUBS)), dma((2, half, SUBS)), dma((nz,)), dma((nz,)),
-                dma((SWEEPS, 2)), dma((SWEEPS, 2)), dma((SWEEPS, 2)),
+                dma((SWEEPS, 2)), dma((SWEEPS, 2)), dma((SWEEPS, 2)), dma((SWEEPS, 2)),
                 dma((2,)), dma((2,)),
                 dma((nz,)), dma((nz,)),
                 dma((2, PARTS, half)), dma((2, PARTS, half)),

time: 146 us -> 149 us (1.021)
  Pallas kernels: 145 us -> 148 us
    pallas_call x1, Pallas kernels: 144 us -> 146 us  [per_device(): pl.pallas_call(functools.partial(kernel, (n_dp, n_proto, rows, feat, cent...]
where the time goes in v4:
time: 149 us
  Pallas kernels  148 us (99%)
    pallas_call x1, Pallas kernels, per_device(): pl.pallas_call(functools.partial(kernel, (n_dp, n_proto, rows, feat, cent...  146 us

profile of v4, /device:TPU:1, one launch (start us, length us, event | category | flops | bytes accessed | tf_op | source)
XLA Modules:
  0.0 148.6 jit_solution(7793888493310376329)
XLA Ops:
  0.6 146.5 %shard_map.41 = (f32[48,512]{1,0:T(8,128)}, f32[1,512]{1,0:T(1,128)}) custom-call(bf16[1536,1536]{1,0:T(8,128)(2,1)} %emb.1, bf16[48,512]{1,0:T(8,128)(2,1)} %bitcast.2), custom_call_target="tpu_custom_call" | custom-call | flops 4831838208 | bytes 4718592 | tf_op jit(solution)/shard_map/pallas_call | solution.py:313
  147.1 1.5 %shard_map.42 = (f32[48,512]{1,0:T(8,128)}, f32[1,512]{1,0:T(1,128)}) custom-call(f32[48,512]{1,0:T(8,128)} %get-tuple-element.6.sums, f32[1,512]{1,0:T(1,128)} %get-tuple-element.7.mass), custom_call_target="tpu_custom_call" | custom-call | tf_op jit(solution)/shard_map/pallas_call | solution.py:345

commit v5 on v2

--- a/solution.py
+++ b/solution.py
@@ -14,7 +14,7 @@
 GROUP = 8
 SUBS = 3
 PARTS = 4
-UNIT = 16
+UNIT = 32
 LANES = 128
 
 
@@ -39,6 +39,8 @@
     other = d + 1 - 2 * c
     right = ((z + 1) % nz) * 2 + c
     left = ((z + nz - 1) % nz) * 2 + c
+    near = (right, left)
+    far = ((d + 4) % n_dp, (d + n_dp - 4) % n_dp)
     in_group = d % GROUP
     level = d // GROUP
     group_ids = [{"dp": level * GROUP + (in_group + j) % GROUP} for j in range(1, GROUP)]
@@ -46,7 +48,7 @@
     proto_ids = [{"proto": (p + j) % n_proto} for j in range(1, n_proto)]
 
     barrier = pltpu.get_barrier_semaphore()
-    partners = [{"dp": left}, {"dp": right}] + group_ids + level_ids + proto_ids
+    partners = [{"dp": t} for t in far + near] + group_ids + level_ids + proto_ids
     for t in partners:
         pl.semaphore_signal(barrier, inc=1, device_id=t, device_id_type=MESH)
 
@@ -60,12 +62,22 @@
     pl.semaphore_wait(barrier, len(partners))
 
     piece = own // SUBS
-
-    def hop(o, way, step, sub):
+    stages = half // 2
+
+    def far_hop(o, way, stage, sub):
         at = ct.at[pl.ds(pl.multiple_of((o * 2 + c) * own + sub * piece, piece), piece)]
         return pltpu.make_async_remote_copy(
-            src_ref=at, dst_ref=at, send_sem=g_send.at[way, step, sub], recv_sem=g_recv.at[way, step, sub],
-            device_id={"dp": right if way == 0 else left}, device_id_type=MESH)
+            src_ref=at, dst_ref=at, send_sem=g_send.at[way, stage, sub], recv_sem=g_recv.at[way, stage, sub],
+            device_id={"dp": far[way]}, device_id_type=MESH)
+
+    def near_hop(o, way, stage):
+        at = ct.at[block_rows(o, c)]
+        return pltpu.make_async_remote_copy(
+            src_ref=at, dst_ref=at, send_sem=g_send.at[way, stage, SUBS], recv_sem=g_recv.at[way, stage, SUBS],
+            device_id={"dp": near[way]}, device_id_type=MESH)
+
+    def source(way, distance):
+        return (z - distance + nz) % nz if way == 0 else (z + distance) % nz
 
     def across(o, slot):
         at = ct.at[block_rows(o, c)]
@@ -80,8 +92,10 @@
         pending.append(desc)
 
     for sub in range(SUBS):
-        launch(hop(z, 0, 0, sub))
-        launch(hop(z, 1, 0, sub))
+        for way in (0, 1):
+            launch(far_hop(z, way, 0, sub))
+    for way in (0, 1):
+        launch(near_hop(z, way, 0))
     launch(across(z, 0))
 
     def square(o, core):
@@ -99,30 +113,40 @@
         v = x[at, :].astype(F32)
         u = (v * (1.0 / jnp.sqrt(jnp.sum(v * v, axis=1, keepdims=True) + 1e-06))).astype(BF16)
         x[at, :] = u
+
+    def turn(b):
+        at = pl.ds(b * short, short)
         for f in range(feat // tile):
             ut[pl.ds(f * tile, tile), at] = dot(
-                eye, u[:, f * tile:(f + 1) * tile], ((1,), (1,))).astype(BF16)
+                eye, x[at, f * tile:(f + 1) * tile], ((1,), (1,))).astype(BF16)
 
     squares = square(z, c)
     behind = [(z, 0)]
     unit = 0
-    for step in range(half):
+    for stage in range(stages):
         came = []
         for sub in range(SUBS):
             if unit < rows // short:
                 prepare(unit)
                 unit += 1
             for way in (0, 1):
-                last = half - 1 if way == 0 else half - 2
-                if step > last:
+                if stage == stages - 1 and way == 1:
                     continue
-                o = (z - 1 - step + nz) % nz if way == 0 else (z + 1 + step) % nz
-                hop(o, way, step, sub).wait_recv()
-                if step < last:
-                    launch(hop(o, way, step + 1, sub))
+                o = source(way, 2 * stage + 2)
+                far_hop(o, way, stage, sub).wait_recv()
+                if stage < stages - 1 and (stage < stages - 2 or way == 0):
+                    launch(far_hop(o, way, stage + 1, sub))
                 if sub == SUBS - 1:
-                    launch(across(o, 1 + 2 * step + way))
-                    came.append((o, 1 + 2 * step + way))
+                    if stage < stages - 1:
+                        launch(near_hop(o, way, stage + 1))
+                    launch(across(o, 2 + 4 * stage + way))
+                    came.append((o, 2 + 4 * stage + way))
+        for way in (0, 1):
+            o = source(way, 2 * stage + 1)
+            near_hop(o, way, stage).wait_recv()
+            slot = 4 * stage + 4 + way if stage < stages - 1 else (1, 2 * half - 1)[way]
+            launch(across(o, slot))
+            came.append((o, slot))
         for o, slot in behind:
             across(o, slot).wait_recv()
             squares = squares + square(o, 1 - c)
@@ -144,7 +168,7 @@
 
     acc = lax.fori_loop(0, 4, score, jnp.zeros((8, cent), F32))
 
-    def exchange(buf, sem, me, ids):
+    def exchange(buf, sem, me, ids, units=()):
         for t in ids:
             pltpu.make_async_remote_copy(
                 src_ref=buf.at[me], dst_ref=buf.at[me], send_sem=sem.at[0], recv_sem=sem.at[1],
@@ -154,19 +178,24 @@
             src_ref=whole, dst_ref=whole, send_sem=sem.at[0], recv_sem=sem.at[1],
             device_id=ids[0], device_id_type=MESH)
         pending.append(done)
+        for b in units:
+            turn(b)
         done.wait_recv()
         return functools.reduce(lambda a, b: a + b, [buf[k] for k in range(len(ids) + 1)])
 
-    def sum_dp(first, second, first_sem, second_sem):
-        second[level] = exchange(first, first_sem, in_group, group_ids)
-        return exchange(second, second_sem, level, level_ids)
+    def sum_dp(first, second, first_sem, second_sem, units=((), ())):
+        second[level] = exchange(first, first_sem, in_group, group_ids, units[0])
+        return exchange(second, second_sem, level, level_ids, units[1])
 
     lane = lax.broadcasted_iota(jnp.int32, (8, LANES), 1)
     tiles = [(0, LANES), (LANES, rows // 8)]
 
+    per_sweep = rows // short // SWEEPS
     for i in range(SWEEPS):
+        turns = range(i * per_sweep, (i + 1) * per_sweep)
         col_a[i, in_group] = jnp.sum(acc, axis=0, keepdims=True)
-        cv = 1.0 / (n_cent * sum_dp(col_a.at[i], col_b.at[i], ca_sem.at[i], cb_sem.at[i]))
+        cv = 1.0 / (n_cent * sum_dp(
+            col_a.at[i], col_b.at[i], ca_sem.at[i], cb_sem.at[i], (turns[0:1], turns[1:2])))
         cb = jnp.broadcast_to(cv, (8, cent))
 
         totals = []
@@ -183,7 +212,7 @@
         row_x[i, p, 0] = totals[0][0:4]
         row_x[i, p, 1] = totals[0][4:8]
         row_x[i, p, 2] = totals[1][0:4] + pltpu.roll(totals[1], LANES // 2, 1)[4:8]
-        rv = 1.0 / (n_rows * exchange(row_x.at[i], rx_sem.at[i], p, proto_ids))
+        rv = 1.0 / (n_rows * exchange(row_x.at[i], rx_sem.at[i], p, proto_ids, turns[2:]))
         r0 = jnp.concatenate([rv[0], rv[1]], axis=0)
         r1 = jnp.concatenate([rv[2], pltpu.roll(rv[2], LANES // 2, 1)], axis=0)
 
@@ -317,7 +346,7 @@
                 vmem((nz, own, cent), F32),
                 vmem((2, PARTS, half + 1, own, cent // PARTS), F32),
                 dma,
-                dma((2, half, SUBS)), dma((2, half, SUBS)), dma((nz,)), dma((nz,)),
+                dma((2, half // 2, SUBS + 1)), dma((2, half // 2, SUBS + 1)), dma((nz,)), dma((nz,)),
                 dma((SWEEPS, 2)), dma((SWEEPS, 2)), dma((SWEEPS, 2)),
                 dma((2,)), dma((2,)),
                 dma((nz,)), dma((nz,)),

time: 146 us -> 134 us (0.918)
  Pallas kernels: 145 us -> 133 us
    pallas_call x1, Pallas kernels: 144 us -> 131 us  [per_device(): pl.pallas_call(functools.partial(kernel, (n_dp, n_proto, rows, feat, cent...]
where the time goes in v5:
time: 134 us
  Pallas kernels  133 us (99%)
    pallas_call x1, Pallas kernels, per_device(): pl.pallas_call(functools.partial(kernel, (n_dp, n_proto, rows, feat, cent...  131 us

profile of v5, /device:TPU:1, one launch (start us, length us, event | category | flops | bytes accessed | tf_op | source)
XLA Modules:
  0.0 133.5 jit_solution(6690664211166176903)
XLA Ops:
  0.6 131.4 %shard_map.41 = (f32[48,512]{1,0:T(8,128)}, f32[1,512]{1,0:T(1,128)}) custom-call(bf16[1536,1536]{1,0:T(8,128)(2,1)} %emb.1, bf16[48,512]{1,0:T(8,128)(2,1)} %bitcast.2), custom_call_target="tpu_custom_call" | custom-call | flops 4831838208 | bytes 4718592 | tf_op jit(solution)/shard_map/pallas_call | solution.py:329
  132.0 1.5 %shard_map.42 = (f32[48,512]{1,0:T(8,128)}, f32[1,512]{1,0:T(1,128)}) custom-call(f32[48,512]{1,0:T(8,128)} %get-tuple-element.6.sums, f32[1,512]{1,0:T(1,128)} %get-tuple-element.7.mass), custom_call_target="tpu_custom_call" | custom-call | tf_op jit(solution)/shard_map/pallas_call | solution.py:360

commit v6 on v5

--- a/solution.py
+++ b/solution.py
@@ -14,6 +14,7 @@
 GROUP = 8
 SUBS = 3
 PARTS = 4
+JOINS = 2
 UNIT = 32
 LANES = 128
 
@@ -22,9 +23,9 @@
     return lax.dot_general(a, b, (dims, ((), ())), preferred_element_type=F32)
 
 
-def kernel(sizes, emb, cen, out, mass_out, x, ut, ct, e, w, s, col_a, col_b, row_x,
-           fin_a, fin_b, sib, ring, sem_in, g_send, g_recv, gs_send, gs_recv, ca_sem, cb_sem, rx_sem,
-           fa_sem, fb_sem, sx_send, sx_recv, r_send, r_recv):
+def kernel(sizes, emb, cen, out, mass_out, x, ut, ct, e, w, s, col_x, row_x, mass_a, mass_b, len_x, sib, leave, ring,
+           sem_in, g_send, g_recv, gs_send, gs_recv, cx_sem, rx_sem, ma_sem, mb_sem, lx_sem,
+           sx_send, sx_recv, r_send, r_recv):
     n_dp, n_proto, rows, feat, cent = sizes
     nz = n_dp // 2
     half = nz // 2
@@ -45,10 +46,11 @@
     level = d // GROUP
     group_ids = [{"dp": level * GROUP + (in_group + j) % GROUP} for j in range(1, GROUP)]
     level_ids = [{"dp": (d + GROUP * j) % n_dp} for j in range(1, levels)]
+    dp_ids = [{"dp": (d + j) % n_dp} for j in sorted(range(1, n_dp), key=lambda j: -min(j, n_dp - j))]
     proto_ids = [{"proto": (p + j) % n_proto} for j in range(1, n_proto)]
 
     barrier = pltpu.get_barrier_semaphore()
-    partners = [{"dp": t} for t in far + near] + group_ids + level_ids + proto_ids
+    partners = dp_ids[::-1] + proto_ids
     for t in partners:
         pl.semaphore_signal(barrier, inc=1, device_id=t, device_id_type=MESH)
 
@@ -168,7 +170,7 @@
 
     acc = lax.fori_loop(0, 4, score, jnp.zeros((8, cent), F32))
 
-    def exchange(buf, sem, me, ids, units=()):
+    def send_all(buf, sem, me, ids):
         for t in ids:
             pltpu.make_async_remote_copy(
                 src_ref=buf.at[me], dst_ref=buf.at[me], send_sem=sem.at[0], recv_sem=sem.at[1],
@@ -178,14 +180,20 @@
             src_ref=whole, dst_ref=whole, send_sem=sem.at[0], recv_sem=sem.at[1],
             device_id=ids[0], device_id_type=MESH)
         pending.append(done)
+        return done
+
+    def total(buf, ids):
+        terms = [buf[k] for k in range(len(ids) + 1)]
+        while len(terms) > 1:
+            terms = [terms[k] + terms[k + 1] for k in range(0, len(terms), 2)]
+        return terms[0]
+
+    def exchange(buf, sem, me, ids, units=()):
+        done = send_all(buf, sem, me, ids)
         for b in units:
             turn(b)
         done.wait_recv()
-        return functools.reduce(lambda a, b: a + b, [buf[k] for k in range(len(ids) + 1)])
-
-    def sum_dp(first, second, first_sem, second_sem, units=((), ())):
-        second[level] = exchange(first, first_sem, in_group, group_ids, units[0])
-        return exchange(second, second_sem, level, level_ids, units[1])
+        return total(buf, ids)
 
     lane = lax.broadcasted_iota(jnp.int32, (8, LANES), 1)
     tiles = [(0, LANES), (LANES, rows // 8)]
@@ -193,9 +201,8 @@
     per_sweep = rows // short // SWEEPS
     for i in range(SWEEPS):
         turns = range(i * per_sweep, (i + 1) * per_sweep)
-        col_a[i, in_group] = jnp.sum(acc, axis=0, keepdims=True)
-        cv = 1.0 / (n_cent * sum_dp(
-            col_a.at[i], col_b.at[i], ca_sem.at[i], cb_sem.at[i], (turns[0:1], turns[1:2])))
+        col_x[i, d] = jnp.sum(acc, axis=0, keepdims=True)
+        cv = 1.0 / (n_cent * exchange(col_x.at[i], cx_sem.at[i], d, dp_ids, turns[0:2]))
         cb = jnp.broadcast_to(cv, (8, cent))
 
         totals = []
@@ -254,55 +261,75 @@
                 first = way == (0 if hops == half else 1)
                 flows.append((way, m if first else PARTS // 2 + m, hops))
 
-    def link(way, part, t):
-        return pltpu.make_async_remote_copy(
-            src_ref=ring.at[way, part, t], dst_ref=ring.at[way, part, t + 1],
-            send_sem=r_send.at[way, part, t], recv_sem=r_recv.at[way, part, t],
-            device_id={"dp": right if way == 0 else left}, device_id_type=MESH)
+    def parent(q, hops):
+        up = (hops - q) // 2
+        return hops - 2 * up - 2 if up < JOINS else q - 1
+
+    def link(way, part, hops, q):
+        step = q - parent(q, hops)
+        return pltpu.make_async_remote_copy(
+            src_ref=leave.at[way, part, q - 1], dst_ref=ring.at[way, part, q - 1],
+            send_sem=r_send.at[way, part, q - 1], recv_sem=r_recv.at[way, part, q - 1],
+            device_id={"dp": (near if step == 1 else far)[way]}, device_id_type=MESH)
 
     own_rows = pl.ds(pl.multiple_of(c * own, own), own)
-
-    def pair_sum(rel, part):
+    ready = set()
+
+    def gathered(way, part, hops, q):
+        rel = (q if way == 0 else nz - q) % nz
+        if rel not in ready:
+            swap(rel).wait_recv()
+            ready.add(rel)
         cols = pl.ds(part * wide, wide)
-        return s[rel, own_rows, cols] + sib[rel, :, cols]
-
-    orders = [[half]] + [[half - q, half + q] for q in range(1, half)] + [[0]]
-    for k in range(3):
-        make_sums(orders[k])
-    ready = set()
-    for t in range(half):
+        v = s[rel, own_rows, cols] + sib[rel, :, cols]
+        return v + children(way, part, hops, q) if q else v
+
+    def children(way, part, hops, q):
+        v = 0.0
+        for child in range(1, hops + 1):
+            if parent(child, hops) == q:
+                link(way, part, hops, child).wait_recv()
+                v = v + ring[way, part, child - 1]
+        return v
+
+    def pass_on(distances):
         for way, part, hops in flows:
-            if t >= hops:
-                continue
-            rel = hops - t if way == 0 else nz - (hops - t)
-            if rel not in ready:
-                swap(rel).wait_recv()
-                ready.add(rel)
-            v = pair_sum(rel, part)
-            if t > 0:
-                link(way, part, t - 1).wait_recv()
-                v = v + ring[way, part, t]
-            ring[way, part, t] = v
-            launch(link(way, part, t))
-        if t + 3 < len(orders):
-            make_sums(orders[t + 3])
-    swap(0).wait_recv()
-    for way, part, hops in flows:
-        link(way, part, hops - 1).wait_recv()
+            for q in distances(hops):
+                leave[way, part, q - 1] = gathered(way, part, hops, q)
+                launch(link(way, part, hops, q))
+
+    mass_a[in_group] = jnp.sum(acc, axis=0, keepdims=True)
+    mass_first = send_all(mass_a, ma_sem, in_group, group_ids)
+    make_sums([half])
+    make_sums([half - 1, half + 1])
+    make_sums([half - 2, half + 2])
+    make_sums([half - 3, half + 3])
+    make_sums([half - 4, half + 4])
+    pass_on(lambda hops: (hops, hops - 1))
+    pass_on(lambda hops: (hops - 3,))
+    mass_first.wait_recv()
+    mass_b[level] = total(mass_a, group_ids)
+    mass_second = send_all(mass_b, mb_sem, level, level_ids)
+    make_sums([half - 5, half + 5])
+    make_sums([half - 6, half + 6])
+    pass_on(lambda hops: (hops - 2,))
+    make_sums([half - 7, half + 7])
+    make_sums([0])
+    for up in range(4, half):
+        pass_on(lambda hops: (hops - up,) if hops > up else ())
     parts = []
     for part in range(PARTS):
-        v = pair_sum(0, part)
+        v = gathered(0, part, half, 0)
         for way, q, hops in flows:
             if q == part:
-                v = v + ring[way, q, hops]
+                v = v + children(way, part, hops, 0)
         parts.append(v)
     sums = jnp.concatenate(parts, axis=1)
-
-    fin_a[in_group, :, 0:cent] = jnp.sum(acc, axis=0, keepdims=True)
-    fin_a[in_group, :, cent:2 * cent] = jnp.sum(sums * sums, axis=0, keepdims=True)
-    tot = sum_dp(fin_a, fin_b, fa_sem, fb_sem)
-    mass_out[...] = n_cent * cv * tot[:, 0:cent]
-    out[...] = sums * (1.0 / jnp.sqrt(tot[:, cent:2 * cent] + 1e-06))
+    len_x[d] = jnp.sum(sums * sums, axis=0, keepdims=True)
+    lengths = exchange(len_x, lx_sem, d, dp_ids)
+    out[...] = sums * (1.0 / jnp.sqrt(lengths + 1e-06))
+    mass_second.wait_recv()
+    mass_out[...] = n_cent * cv * total(mass_b, level_ids)
 
     for desc in pending:
         desc.wait_send()
@@ -338,17 +365,17 @@
                 vmem((rows, cent), F32),
                 vmem((rows, cent), BF16),
                 vmem((nz, 2 * own, cent), F32),
-                vmem((SWEEPS, GROUP, 1, cent), F32),
-                vmem((SWEEPS, levels, 1, cent), F32),
+                vmem((SWEEPS, n_dp, 1, cent), F32),
                 vmem((SWEEPS, n_proto, 3, 4, LANES), F32),
-                vmem((GROUP, 1, 2 * cent), F32),
-                vmem((levels, 1, 2 * cent), F32),
+                vmem((GROUP, 1, cent), F32),
+                vmem((levels, 1, cent), F32),
+                vmem((n_dp, 1, cent), F32),
                 vmem((nz, own, cent), F32),
-                vmem((2, PARTS, half + 1, own, cent // PARTS), F32),
+                vmem((2, PARTS, half, own, cent // PARTS), F32),
+                vmem((2, PARTS, half, own, cent // PARTS), F32),
                 dma,
                 dma((2, half // 2, SUBS + 1)), dma((2, half // 2, SUBS + 1)), dma((nz,)), dma((nz,)),
-                dma((SWEEPS, 2)), dma((SWEEPS, 2)), dma((SWEEPS, 2)),
-                dma((2,)), dma((2,)),
+                dma((SWEEPS, 2)), dma((SWEEPS, 2)), dma((2,)), dma((2,)), dma((2,)),
                 dma((nz,)), dma((nz,)),
                 dma((2, PARTS, half)), dma((2, PARTS, half)),
             ],

time: 134 us -> 123 us (0.918)
  Pallas kernels: 133 us -> 122 us
    pallas_call x1, Pallas kernels: 131 us -> 120 us  [per_device(): pl.pallas_call(functools.partial(kernel, (n_dp, n_proto, rows, feat, cent...]
where the time goes in v6:
time: 123 us; the launch traced here: 122 us
  Pallas kernels  122 us (99%)
    pallas_call x1, Pallas kernels, per_device(): pl.pallas_call(functools.partial(kernel, (n_dp, n_proto, rows, feat, cent...  120 us

profile of v6, /device:TPU:1, one launch (start us, length us, event | category | flops | bytes accessed | tf_op | source)
XLA Modules:
  0.0 122.4 jit_solution(9093511764739572098)
XLA Ops:
  0.6 120.2 %shard_map.41 = (f32[48,512]{1,0:T(8,128)}, f32[1,512]{1,0:T(1,128)}) custom-call(bf16[1536,1536]{1,0:T(8,128)(2,1)} %emb.1, bf16[48,512]{1,0:T(8,128)(2,1)} %bitcast.2), custom_call_target="tpu_custom_call" | custom-call | flops 4831838208 | bytes 4718592 | tf_op jit(solution)/shard_map/pallas_call | solution.py:356
  120.8 1.5 %shard_map.42 = (f32[48,512]{1,0:T(8,128)}, f32[1,512]{1,0:T(1,128)}) custom-call(f32[48,512]{1,0:T(8,128)} %get-tuple-element.6.sums, f32[1,512]{1,0:T(1,128)} %get-tuple-element.7.mass), custom_call_target="tpu_custom_call" | custom-call | tf_op jit(solution)/shard_map/pallas_call | solution.py:387

commit v7 on v6

--- a/solution.py
+++ b/solution.py
@@ -24,7 +24,7 @@
 
 
 def kernel(sizes, emb, cen, out, mass_out, x, ut, ct, e, w, s, col_x, row_x, mass_a, mass_b, len_x, sib, leave, ring,
-           sem_in, g_send, g_recv, gs_send, gs_recv, cx_sem, rx_sem, ma_sem, mb_sem, lx_sem,
+           sem_in, g_send, g_recv, gs_recv, cx_sem, rx_sem, ma_sem, mb_sem, lx_sem,
            sx_send, sx_recv, r_send, r_recv):
     n_dp, n_proto, rows, feat, cent = sizes
     nz = n_dp // 2
@@ -49,14 +49,14 @@
     dp_ids = [{"dp": (d + j) % n_dp} for j in sorted(range(1, n_dp), key=lambda j: -min(j, n_dp - j))]
     proto_ids = [{"proto": (p + j) % n_proto} for j in range(1, n_proto)]
 
+    load = pltpu.make_async_copy(emb, x, sem_in)
+    load.start()
+
     barrier = pltpu.get_barrier_semaphore()
     partners = dp_ids[::-1] + proto_ids
     for t in partners:
         pl.semaphore_signal(barrier, inc=1, device_id=t, device_id_type=MESH)
 
-    load = pltpu.make_async_copy(emb, x, sem_in)
-    load.start()
-
     def block_rows(o, core):
         return pl.ds(pl.multiple_of((o * 2 + core) * own, own), own)
 
@@ -69,13 +69,13 @@
     def far_hop(o, way, stage, sub):
         at = ct.at[pl.ds(pl.multiple_of((o * 2 + c) * own + sub * piece, piece), piece)]
         return pltpu.make_async_remote_copy(
-            src_ref=at, dst_ref=at, send_sem=g_send.at[way, stage, sub], recv_sem=g_recv.at[way, stage, sub],
+            src_ref=at, dst_ref=at, send_sem=g_send, recv_sem=g_recv.at[way, stage, sub],
             device_id={"dp": far[way]}, device_id_type=MESH)
 
     def near_hop(o, way, stage):
         at = ct.at[block_rows(o, c)]
         return pltpu.make_async_remote_copy(
-            src_ref=at, dst_ref=at, send_sem=g_send.at[way, stage, SUBS], recv_sem=g_recv.at[way, stage, SUBS],
+            src_ref=at, dst_ref=at, send_sem=g_send, recv_sem=g_recv.at[way, stage, SUBS],
             device_id={"dp": near[way]}, device_id_type=MESH)
 
     def source(way, distance):
@@ -84,14 +84,13 @@
     def across(o, slot):
         at = ct.at[block_rows(o, c)]
         return pltpu.make_async_remote_copy(
-            src_ref=at, dst_ref=at, send_sem=gs_send.at[slot], recv_sem=gs_recv.at[slot],
+            src_ref=at, dst_ref=at, send_sem=g_send, recv_sem=gs_recv.at[slot],
             device_id={"dp": other}, device_id_type=MESH)
 
     pending = []
 
     def launch(desc):
         desc.start()
-        pending.append(desc)
 
     for sub in range(SUBS):
         for way in (0, 1):
@@ -162,13 +161,17 @@
     scale = LOGIT_SCALE * (1.0 / jnp.sqrt(jnp.sum(squares, axis=0, keepdims=True) + 1e-06))
     m_tile = rows // 4
 
-    def score(b, acc):
-        at = pl.ds(pl.multiple_of(b * m_tile, m_tile), m_tile)
-        v = jnp.exp(dot(x[at, :], ct[...], ((1,), (0,))) * scale)
-        e[at, :] = v
-        return acc + jnp.sum(v.reshape(m_tile // 8, 8, cent), axis=0)
-
-    acc = lax.fori_loop(0, 4, score, jnp.zeros((8, cent), F32))
+    def product(b):
+        return dot(x[b * m_tile:(b + 1) * m_tile, :], ct[...], ((1,), (0,)))
+
+    acc = jnp.zeros((8, cent), F32)
+    raw = product(0)
+    for b in range(4):
+        ahead = product(b + 1) if b < 3 else None
+        v = jnp.exp(raw * scale)
+        e[b * m_tile:(b + 1) * m_tile, :] = v
+        acc = acc + jnp.sum(v.reshape(m_tile // 8, 8, cent), axis=0)
+        raw = ahead
 
     def send_all(buf, sem, me, ids):
         for t in ids:
@@ -188,10 +191,12 @@
             terms = [terms[k] + terms[k + 1] for k in range(0, len(terms), 2)]
         return terms[0]
 
-    def exchange(buf, sem, me, ids, units=()):
+    def exchange(buf, sem, me, ids, units=(), drain=None):
         done = send_all(buf, sem, me, ids)
         for b in units:
             turn(b)
+        if drain:
+            drain()
         done.wait_recv()
         return total(buf, ids)
 
@@ -243,7 +248,7 @@
     def swap(rel):
         return pltpu.make_async_remote_copy(
             src_ref=s.at[rel, pl.ds(pl.multiple_of((1 - c) * own, own), own)], dst_ref=sib.at[rel],
-            send_sem=sx_send.at[rel], recv_sem=sx_recv.at[rel],
+            send_sem=sx_send, recv_sem=sx_recv.at[rel],
             device_id={"dp": other}, device_id_type=MESH)
 
     def make_sums(rels):
@@ -269,7 +274,7 @@
         step = q - parent(q, hops)
         return pltpu.make_async_remote_copy(
             src_ref=leave.at[way, part, q - 1], dst_ref=ring.at[way, part, q - 1],
-            send_sem=r_send.at[way, part, q - 1], recv_sem=r_recv.at[way, part, q - 1],
+            send_sem=r_send, recv_sem=r_recv.at[way, part, q - 1],
             device_id={"dp": (near if step == 1 else far)[way]}, device_id_type=MESH)
 
     own_rows = pl.ds(pl.multiple_of(c * own, own), own)
@@ -326,18 +331,29 @@
         parts.append(v)
     sums = jnp.concatenate(parts, axis=1)
     len_x[d] = jnp.sum(sums * sums, axis=0, keepdims=True)
-    lengths = exchange(len_x, lx_sem, d, dp_ids)
+
+    def drain():
+        for ref, sem in ((ct.at[pl.ds(0, (2 * nz - 1) * own)], g_send), (sib, sx_send),
+                         (sib.at[pl.ds(0, nz - 1)], r_send)):
+            pltpu.make_async_remote_copy(
+                src_ref=ref, dst_ref=ref, send_sem=sem, recv_sem=sem,
+                device_id={"dp": other}, device_id_type=MESH).wait_send()
+        for desc in pending:
+            desc.wait_send()
+        pending.clear()
+
+    lengths = exchange(len_x, lx_sem, d, dp_ids, drain=drain)
     out[...] = sums * (1.0 / jnp.sqrt(lengths + 1e-06))
     mass_second.wait_recv()
     mass_out[...] = n_cent * cv * total(mass_b, level_ids)
 
-    for desc in pending:
-        desc.wait_send()
-
-
-def hand_over(sums, mass, sums_out, mass_out):
-    sums_out[...] = sums[...]
-    mass_out[...] = mass[...]
+
+def hand_over(sums, mass, sums_out, mass_out, sems):
+    copies = [pltpu.make_async_copy(sums, sums_out, sems.at[0]), pltpu.make_async_copy(mass, mass_out, sems.at[1])]
+    for copy in copies:
+        copy.start()
+    for copy in copies:
+        copy.wait()
 
 
 def solution(mesh):
@@ -351,12 +367,12 @@
         cent = centroids.shape[0]
         own = feat // n_dp
         dma, vmem = pltpu.SemaphoreType.DMA, pltpu.VMEM
-        whole = pl.BlockSpec(memory_space=pltpu.VMEM)
+        whole, anywhere = pl.BlockSpec(memory_space=pltpu.VMEM), pl.BlockSpec(memory_space=pl.ANY)
         shapes = (jax.ShapeDtypeStruct((own, cent), F32), jax.ShapeDtypeStruct((1, cent), F32))
         sums, mass = pl.pallas_call(
             functools.partial(kernel, (n_dp, n_proto, rows, feat, cent)),
             out_shape=shapes,
-            in_specs=[pl.BlockSpec(memory_space=pl.ANY), whole],
+            in_specs=[anywhere, whole],
             out_specs=(whole, whole),
             scratch_shapes=[
                 vmem((rows, feat), BF16),
@@ -374,10 +390,9 @@
                 vmem((2, PARTS, half, own, cent // PARTS), F32),
                 vmem((2, PARTS, half, own, cent // PARTS), F32),
                 dma,
-                dma((2, half // 2, SUBS + 1)), dma((2, half // 2, SUBS + 1)), dma((nz,)), dma((nz,)),
+                dma, dma((2, half // 2, SUBS + 1)), dma((nz,)),
                 dma((SWEEPS, 2)), dma((SWEEPS, 2)), dma((2,)), dma((2,)), dma((2,)),
-                dma((nz,)), dma((nz,)),
-                dma((2, PARTS, half)), dma((2, PARTS, half)),
+                dma, dma((nz,)), dma, dma((2, PARTS, half)),
             ],
             compiler_params=pltpu.CompilerParams(
                 collective_id=0, has_side_effects=True, vmem_limit_bytes=56 * 1024 * 1024),
@@ -385,7 +400,8 @@
                 flops=4 * rows * feat * cent, bytes_accessed=2 * rows * feat, transcendentals=rows * cent),
         )(embeddings, centroids.T)
         new_centroids, mass = pl.pallas_call(
-            hand_over, out_shape=shapes, in_specs=[whole, whole], out_specs=(whole, whole))(sums, mass)
+            hand_over, out_shape=shapes, in_specs=[anywhere, anywhere], out_specs=(anywhere, anywhere),
+            scratch_shapes=[dma((2,))])(sums, mass)
         return new_centroids, mass.reshape(cent)
 
     return jax.shard_map(

time: 123 us -> 124 us (level)
    pallas_call x1, Pallas kernels: 1.55 us -> 4.16 us  [per_device(): pl.pallas_call(hand_over, out_shape=shapes, in_specs=[anywhere, anywhere]...]
    pallas_call x1, Pallas kernels: 120 us -> 118 us  [per_device(): pl.pallas_call(functools.partial(kernel, (n_dp, n_proto, rows, feat, cent...]
where the time goes in v7:
time: 124 us; the launch traced here: 123 us
  Pallas kernels  123 us (99%)
    pallas_call x1, Pallas kernels, per_device(): pl.pallas_call(functools.partial(kernel, (n_dp, n_proto, rows, feat, cent...  118 us
    pallas_call x1, Pallas kernels, per_device(): pl.pallas_call(hand_over, out_shape=shapes, in_specs=[anywhere, anywhere]...  4.16 us

profile of v7, /device:TPU:1, one launch (start us, length us, event | category | flops | bytes accessed | tf_op | source)
XLA Modules:
  0.0 123.4 jit_solution(13934420091077925885)
XLA Ops:
  0.6 118.5 %shard_map.41 = (f32[48,512]{1,0:T(8,128)}, f32[1,512]{1,0:T(1,128)}) custom-call(bf16[1536,1536]{1,0:T(8,128)(2,1)} %emb.1, bf16[48,512]{1,0:T(8,128)(2,1)} %bitcast.2), custom_call_target="tpu_custom_call" | custom-call | flops 4831838208 | bytes 4718592 | tf_op jit(solution)/shard_map/pallas_call | solution.py:372
  119.1 4.2 %shard_map.42 = (f32[48,512]{1,0:T(8,128)}, f32[1,512]{1,0:T(1,128)}) custom-call(f32[48,512]{1,0:T(8,128)} %get-tuple-element.6.sums, f32[1,512]{1,0:T(1,128)} %get-tuple-element.7.mass), custom_call_target="tpu_custom_call" | custom-call | tf_op jit(solution)/shard_map/pallas_call | solution.py:402

commit v8 on v7

--- a/solution.py
+++ b/solution.py
@@ -15,7 +15,7 @@
 SUBS = 3
 PARTS = 4
 JOINS = 2
-UNIT = 32
+UNIT = 64
 LANES = 128
 
 
@@ -47,7 +47,10 @@
     group_ids = [{"dp": level * GROUP + (in_group + j) % GROUP} for j in range(1, GROUP)]
     level_ids = [{"dp": (d + GROUP * j) % n_dp} for j in range(1, levels)]
     dp_ids = [{"dp": (d + j) % n_dp} for j in sorted(range(1, n_dp), key=lambda j: -min(j, n_dp - j))]
-    proto_ids = [{"proto": (p + j) % n_proto} for j in range(1, n_proto)]
+    side = int(n_proto**0.5)
+    moves = [(a, b) for a in range(side) for b in range(side) if a or b]
+    moves.sort(key=lambda m: -sum(min(k, side - k) for k in m))
+    proto_ids = [{"proto": (p // side + a) % side * side + (p % side + b) % side} for a, b in moves]
 
     load = pltpu.make_async_copy(emb, x, sem_in)
     load.start()
@@ -126,10 +129,10 @@
     unit = 0
     for stage in range(stages):
         came = []
+        for _ in range(rows // short // stages):
+            prepare(unit)
+            unit += 1
         for sub in range(SUBS):
-            if unit < rows // short:
-                prepare(unit)
-                unit += 1
             for way in (0, 1):
                 if stage == stages - 1 and way == 1:
                     continue
@@ -348,12 +351,9 @@
     mass_out[...] = n_cent * cv * total(mass_b, level_ids)
 
 
-def hand_over(sums, mass, sums_out, mass_out, sems):
-    copies = [pltpu.make_async_copy(sums, sums_out, sems.at[0]), pltpu.make_async_copy(mass, mass_out, sems.at[1])]
-    for copy in copies:
-        copy.start()
-    for copy in copies:
-        copy.wait()
+def hand_over(sums, mass, sums_out, mass_out):
+    sums_out[...] = sums[...]
+    mass_out[...] = mass[...]
 
 
 def solution(mesh):
@@ -400,8 +400,7 @@
                 flops=4 * rows * feat * cent, bytes_accessed=2 * rows * feat, transcendentals=rows * cent),
         )(embeddings, centroids.T)
         new_centroids, mass = pl.pallas_call(
-            hand_over, out_shape=shapes, in_specs=[anywhere, anywhere], out_specs=(anywhere, anywhere),
-            scratch_shapes=[dma((2,))])(sums, mass)
+            hand_over, out_shape=shapes, in_specs=[whole, whole], out_specs=(whole, whole))(sums, mass)
         return new_centroids, mass.reshape(cent)
 
     return jax.shard_map(

time: 124 us -> 120 us (0.968)
  Pallas kernels: 123 us -> 119 us
    pallas_call x1, Pallas kernels: 4.16 us -> 1.55 us  [per_device(): pl.pallas_call(hand_over, out_shape=shapes, in_specs=[whole, whole], out_...]
    pallas_call x1, Pallas kernels: 118 us -> 117 us  [per_device(): pl.pallas_call(functools.partial(kernel, (n_dp, n_proto, rows, feat, cent...]
where the time goes in v8:
time: 120 us; the launch traced here: 119 us
  Pallas kernels  119 us (99%)
    pallas_call x1, Pallas kernels, per_device(): pl.pallas_call(functools.partial(kernel, (n_dp, n_proto, rows, feat, cent...  117 us

profile of v8, /device:TPU:1, one launch (start us, length us, event | category | flops | bytes accessed | tf_op | source)
XLA Modules:
  0.0 119.3 jit_solution(4006071704778153415)
XLA Ops:
  0.6 117.1 %shard_map.41 = (f32[48,512]{1,0:T(8,128)}, f32[1,512]{1,0:T(1,128)}) custom-call(bf16[1536,1536]{1,0:T(8,128)(2,1)} %emb.1, bf16[48,512]{1,0:T(8,128)(2,1)} %bitcast.2), custom_call_target="tpu_custom_call" | custom-call | flops 4831838208 | bytes 4718592 | tf_op jit(solution)/shard_map/pallas_call | solution.py:372
  117.8 1.5 %shard_map.42 = (f32[48,512]{1,0:T(8,128)}, f32[1,512]{1,0:T(1,128)}) custom-call(f32[48,512]{1,0:T(8,128)} %get-tuple-element.6.sums, f32[1,512]{1,0:T(1,128)} %get-tuple-element.7.mass), custom_call_target="tpu_custom_call" | custom-call | tf_op jit(solution)/shard_map/pallas_call | solution.py:402

commit v9 on v8

--- a/solution.py
+++ b/solution.py
@@ -14,7 +14,7 @@
 GROUP = 8
 SUBS = 3
 PARTS = 4
-JOINS = 2
+JOINS = 3
 UNIT = 64
 LANES = 128
 
@@ -56,7 +56,7 @@
     load.start()
 
     barrier = pltpu.get_barrier_semaphore()
-    partners = dp_ids[::-1] + proto_ids
+    partners = [{"dp": t} for t in near + far + (other,)] + proto_ids
     for t in partners:
         pl.semaphore_signal(barrier, inc=1, device_id=t, device_id_type=MESH)
 
@@ -321,9 +321,10 @@
     make_sums([half - 5, half + 5])
     make_sums([half - 6, half + 6])
     pass_on(lambda hops: (hops - 2,))
+    pass_on(lambda hops: (hops - 5,))
     make_sums([half - 7, half + 7])
     make_sums([0])
-    for up in range(4, half):
+    for up in (4, 6, 7):
         pass_on(lambda hops: (hops - up,) if hops > up else ())
     parts = []
     for part in range(PARTS):

time: 120 us -> 116 us (0.967)
  Pallas kernels: 119 us -> 115 us
    pallas_call x1, Pallas kernels: 117 us -> 113 us  [per_device(): pl.pallas_call(functools.partial(kernel, (n_dp, n_proto, rows, feat, cent...]
where the time goes in v9:
time: 116 us; the launch traced here: 115 us
  Pallas kernels  115 us (99%)
    pallas_call x1, Pallas kernels, per_device(): pl.pallas_call(functools.partial(kernel, (n_dp, n_proto, rows, feat, cent...  113 us

profile of v9, /device:TPU:1, one launch (start us, length us, event | category | flops | bytes accessed | tf_op | source)
XLA Modules:
  0.0 115.4 jit_solution(5682975247686636570)
XLA Ops:
  0.6 113.2 %shard_map.41 = (f32[48,512]{1,0:T(8,128)}, f32[1,512]{1,0:T(1,128)}) custom-call(bf16[1536,1536]{1,0:T(8,128)(2,1)} %emb.1, bf16[48,512]{1,0:T(8,128)(2,1)} %bitcast.2), custom_call_target="tpu_custom_call" | custom-call | flops 4831838208 | bytes 4718592 | tf_op jit(solution)/shard_map/pallas_call | solution.py:373
  113.8 1.5 %shard_map.42 = (f32[48,512]{1,0:T(8,128)}, f32[1,512]{1,0:T(1,128)}) custom-call(f32[48,512]{1,0:T(8,128)} %get-tuple-element.6.sums, f32[1,512]{1,0:T(1,128)} %get-tuple-element.7.mass), custom_call_target="tpu_custom_call" | custom-call | tf_op jit(solution)/shard_map/pallas_call | solution.py:403

commit v10 on v9

--- a/solution.py
+++ b/solution.py
@@ -14,7 +14,8 @@
 GROUP = 8
 SUBS = 3
 PARTS = 4
-JOINS = 3
+JOINS = 4
+LOADS = 3
 UNIT = 64
 LANES = 128
 
@@ -52,8 +53,11 @@
     moves.sort(key=lambda m: -sum(min(k, side - k) for k in m))
     proto_ids = [{"proto": (p // side + a) % side * side + (p % side + b) % side} for a, b in moves]
 
-    load = pltpu.make_async_copy(emb, x, sem_in)
-    load.start()
+    loads = []
+    for k in range(LOADS):
+        chunk = pl.ds(k * (rows // LOADS), rows // LOADS)
+        loads.append(pltpu.make_async_copy(emb.at[chunk], x.at[chunk], sem_in.at[k]))
+        loads[k].start()
 
     barrier = pltpu.get_barrier_semaphore()
     partners = [{"dp": t} for t in near + far + (other,)] + proto_ids
@@ -106,7 +110,6 @@
         v = ct[block_rows(o, core), :].astype(F32)
         return jnp.sum((v * v).reshape(own // 8, 8, cent), axis=0)
 
-    load.wait()
     tile, short = 256, 128
     eye = (
         lax.broadcasted_iota(jnp.int32, (tile, tile), 0) == lax.broadcasted_iota(jnp.int32, (tile, tile), 1)
@@ -129,9 +132,11 @@
     unit = 0
     for stage in range(stages):
         came = []
-        for _ in range(rows // short // stages):
-            prepare(unit)
-            unit += 1
+        if stage > 0:
+            loads[stage - 1].wait()
+            for _ in range(rows // short // LOADS):
+                prepare(unit)
+                unit += 1
         for sub in range(SUBS):
             for way in (0, 1):
                 if stage == stages - 1 and way == 1:
@@ -271,7 +276,7 @@
 
     def parent(q, hops):
         up = (hops - q) // 2
-        return hops - 2 * up - 2 if up < JOINS else q - 1
+        return max(hops - 2 * up - 2, 0) if up < JOINS else q - 1
 
     def link(way, part, hops, q):
         step = q - parent(q, hops)
@@ -324,7 +329,7 @@
     pass_on(lambda hops: (hops - 5,))
     make_sums([half - 7, half + 7])
     make_sums([0])
-    for up in (4, 6, 7):
+    for up in (4, 7, 6):
         pass_on(lambda hops: (hops - up,) if hops > up else ())
     parts = []
     for part in range(PARTS):
@@ -390,7 +395,7 @@
                 vmem((nz, own, cent), F32),
                 vmem((2, PARTS, half, own, cent // PARTS), F32),
                 vmem((2, PARTS, half, own, cent // PARTS), F32),
-                dma,
+                dma((LOADS,)),
                 dma, dma((2, half // 2, SUBS + 1)), dma((nz,)),
                 dma((SWEEPS, 2)), dma((SWEEPS, 2)), dma((2,)), dma((2,)), dma((2,)),
                 dma, dma((nz,)), dma, dma((2, PARTS, half)),

time: 116 us -> 114 us (0.983)
  Pallas kernels: 115 us -> 113 us
    pallas_call x1, Pallas kernels: 113 us -> 112 us  [per_device(): pl.pallas_call(functools.partial(kernel, (n_dp, n_proto, rows, feat, cent...]
where the time goes in v10:
time: 114 us
  Pallas kernels  113 us (99%)
    pallas_call x1, Pallas kernels, per_device(): pl.pallas_call(functools.partial(kernel, (n_dp, n_proto, rows, feat, cent...  112 us

profile of v10, /device:TPU:1, one launch (start us, length us, event | category | flops | bytes accessed | tf_op | source)
XLA Modules:
  0.0 114.0 jit_solution(4120679241636326115)
XLA Ops:
  0.6 111.8 %shard_map.41 = (f32[48,512]{1,0:T(8,128)}, f32[1,512]{1,0:T(1,128)}) custom-call(bf16[1536,1536]{1,0:T(8,128)(2,1)} %emb.1, bf16[48,512]{1,0:T(8,128)(2,1)} %bitcast.2), custom_call_target="tpu_custom_call" | custom-call | flops 4831838208 | bytes 4718592 | tf_op jit(solution)/shard_map/pallas_call | solution.py:378
  112.5 1.5 %shard_map.42 = (f32[48,512]{1,0:T(8,128)}, f32[1,512]{1,0:T(1,128)}) custom-call(f32[48,512]{1,0:T(8,128)} %get-tuple-element.6.sums, f32[1,512]{1,0:T(1,128)} %get-tuple-element.7.mass), custom_call_target="tpu_custom_call" | custom-call | tf_op jit(solution)/shard_map/pallas_call | solution.py:408

commit v11 on v10

--- a/solution.py
+++ b/solution.py
@@ -14,7 +14,7 @@
 GROUP = 8
 SUBS = 3
 PARTS = 4
-JOINS = 4
+DEPTH = 5
 LOADS = 3
 UNIT = 64
 LANES = 128
@@ -130,6 +130,7 @@
     squares = square(z, c)
     behind = [(z, 0)]
     unit = 0
+    opposite = ((0, 1), (2,))
     for stage in range(stages):
         came = []
         if stage > 0:
@@ -139,17 +140,18 @@
                 unit += 1
         for sub in range(SUBS):
             for way in (0, 1):
-                if stage == stages - 1 and way == 1:
+                if stage == stages - 1 and sub not in opposite[way]:
                     continue
                 o = source(way, 2 * stage + 2)
                 far_hop(o, way, stage, sub).wait_recv()
-                if stage < stages - 1 and (stage < stages - 2 or way == 0):
+                if stage < stages - 1 and (stage < stages - 2 or sub in opposite[way]):
                     launch(far_hop(o, way, stage + 1, sub))
                 if sub == SUBS - 1:
                     if stage < stages - 1:
                         launch(near_hop(o, way, stage + 1))
-                    launch(across(o, 2 + 4 * stage + way))
-                    came.append((o, 2 + 4 * stage + way))
+                    slot = 2 + 4 * stage + (way if stage < stages - 1 else 0)
+                    launch(across(o, slot))
+                    came.append((o, slot))
         for way in (0, 1):
             o = source(way, 2 * stage + 1)
             near_hop(o, way, stage).wait_recv()
@@ -276,7 +278,7 @@
 
     def parent(q, hops):
         up = (hops - q) // 2
-        return max(hops - 2 * up - 2, 0) if up < JOINS else q - 1
+        return hops - 2 * up - 2 if up < hops - DEPTH else q - 1
 
     def link(way, part, hops, q):
         step = q - parent(q, hops)
@@ -326,11 +328,12 @@
     make_sums([half - 5, half + 5])
     make_sums([half - 6, half + 6])
     pass_on(lambda hops: (hops - 2,))
-    pass_on(lambda hops: (hops - 5,))
+    pass_on(lambda hops: (3,) if hops == half else ())
     make_sums([half - 7, half + 7])
     make_sums([0])
-    for up in (4, 7, 6):
-        pass_on(lambda hops: (hops - up,) if hops > up else ())
+    pass_on(lambda hops: (hops - 4,))
+    pass_on(lambda hops: (2,))
+    pass_on(lambda hops: (1,))
     parts = []
     for part in range(PARTS):
         v = gathered(0, part, half, 0)

time: 114 us -> 116 us (1.018)
  Pallas kernels: 113 us -> 115 us
    pallas_call x1, Pallas kernels: 112 us -> 114 us  [per_device(): pl.pallas_call(functools.partial(kernel, (n_dp, n_proto, rows, feat, cent...]
where the time goes in v11:
time: 116 us
  Pallas kernels  115 us (99%)
    pallas_call x1, Pallas kernels, per_device(): pl.pallas_call(functools.partial(kernel, (n_dp, n_proto, rows, feat, cent...  114 us

profile of v11, /device:TPU:1, one launch (start us, length us, event | category | flops | bytes accessed | tf_op | source)
XLA Modules:
  0.0 115.9 jit_solution(11776310780619744774)
XLA Ops:
  0.6 113.7 %shard_map.41 = (f32[48,512]{1,0:T(8,128)}, f32[1,512]{1,0:T(1,128)}) custom-call(bf16[1536,1536]{1,0:T(8,128)(2,1)} %emb.1, bf16[48,512]{1,0:T(8,128)(2,1)} %bitcast.2), custom_call_target="tpu_custom_call" | custom-call | flops 4831838208 | bytes 4718592 | tf_op jit(solution)/shard_map/pallas_call | solution.py:381
  114.3 1.5 %shard_map.42 = (f32[48,512]{1,0:T(8,128)}, f32[1,512]{1,0:T(1,128)}) custom-call(f32[48,512]{1,0:T(8,128)} %get-tuple-element.6.sums, f32[1,512]{1,0:T(1,128)} %get-tuple-element.7.mass), custom_call_target="tpu_custom_call" | custom-call | tf_op jit(solution)/shard_map/pallas_call | solution.py:411

commit v12 on v10

--- a/solution.py
+++ b/solution.py
@@ -167,15 +167,15 @@
         squares = squares + square(o, 1 - c)
 
     scale = LOGIT_SCALE * (1.0 / jnp.sqrt(jnp.sum(squares, axis=0, keepdims=True) + 1e-06))
-    m_tile = rows // 4
+    m_tile = rows // 2
 
     def product(b):
         return dot(x[b * m_tile:(b + 1) * m_tile, :], ct[...], ((1,), (0,)))
 
     acc = jnp.zeros((8, cent), F32)
     raw = product(0)
-    for b in range(4):
-        ahead = product(b + 1) if b < 3 else None
+    for b in range(2):
+        ahead = product(b + 1) if b < 1 else None
         v = jnp.exp(raw * scale)
         e[b * m_tile:(b + 1) * m_tile, :] = v
         acc = acc + jnp.sum(v.reshape(m_tile // 8, 8, cent), axis=0)

time: 114 us -> 114 us (level)
  no operation moved by 1% of the time
where the time goes in v12:
time: 114 us
  Pallas kernels  113 us (99%)
    pallas_call x1, Pallas kernels, per_device(): pl.pallas_call(functools.partial(kernel, (n_dp, n_proto, rows, feat, cent...  112 us

profile of v12, /device:TPU:1, one launch (start us, length us, event | category | flops | bytes accessed | tf_op | source)
XLA Modules:
  0.0 114.0 jit_solution(10651596769141724709)
XLA Ops:
  0.6 111.8 %shard_map.41 = (f32[48,512]{1,0:T(8,128)}, f32[1,512]{1,0:T(1,128)}) custom-call(bf16[1536,1536]{1,0:T(8,128)(2,1)} %emb.1, bf16[48,512]{1,0:T(8,128)(2,1)} %bitcast.2), custom_call_target="tpu_custom_call" | custom-call | flops 4831838208 | bytes 4718592 | tf_op jit(solution)/shard_map/pallas_call | solution.py:378
  112.4 1.5 %shard_map.42 = (f32[48,512]{1,0:T(8,128)}, f32[1,512]{1,0:T(1,128)}) custom-call(f32[48,512]{1,0:T(8,128)} %get-tuple-element.6.sums, f32[1,512]{1,0:T(1,128)} %get-tuple-element.7.mass), custom_call_target="tpu_custom_call" | custom-call | tf_op jit(solution)/shard_map/pallas_call | solution.py:408
